TPU v7x, 256 devices: a whole 4x4x8 slice. The times are simulated.
256 devices in a mesh: rows: 64 (over z, y, core), heads: 4 (over x).
Axes of the slice: x: 4, y: 4, z: 8, core: 2. Of those that a mesh axis runs over, the one named last changes fastest.
Arguments:
- row_layer_input: bfloat16 [256, 64, 768], P('rows'), may hold values from -6 to 6
- column_layer_input: bfloat16 [256, 64, 768], P('rows'), may hold values from -6 to 6
- feedforward_layer_input: bfloat16 [256, 64, 768], P('rows'), may hold values from -6 to 6
- grad_out: bfloat16 [256, 64, 768], P('rows'), may hold values from -16 to 16
- layer_norm_gains: float32 [3, 768], replicated, may hold values from 0.25 to 1.75
- row_qkv: bfloat16 [768, 3, 768], P(None, None, 'heads'), may hold values from -0.21875 to 0.21875
- row_out: bfloat16 [768, 768], P(None, 'heads'), may hold values from -0.21875 to 0.21875
- col_qkv: bfloat16 [768, 3, 768], P(None, None, 'heads'), may hold values from -0.21875 to 0.21875
- col_out: bfloat16 [768, 768], P(None, 'heads'), may hold values from -0.21875 to 0.21875
- ffn_up: bfloat16 [768, 3072], P(None, 'heads'), may hold values from -0.21875 to 0.21875
- ffn_down: bfloat16 [768, 3072], P(None, 'heads'), may hold values from -0.109375 to 0.109375
Outputs:
- input_gradient: bfloat16 [256, 64, 768], P('rows')
- grad_row_qkv: float32 [768, 3, 768], P('rows', None, 'heads')
- grad_row_out: float32 [768, 768], P('rows', 'heads')
- grad_col_qkv: float32 [768, 3, 768], P('rows', None, 'heads')
- grad_col_out: float32 [768, 768], P('rows', 'heads')
- grad_ffn_up: float32 [768, 3072], P('rows', 'heads')
- grad_ffn_down: float32 [768, 3072], P('rows', 'heads')
All inputs are finite; a program needn't handle non-finite values.
Results may differ from a plain program's by a relative error of at most 0.028.
Values may be sent and summed in bfloat16 or wider, within the bound.
No kernel may reach another device: no remote copies, remote signals or barrier semaphores. Data moves between devices by JAX's collectives and lax.ppermute only.
A program may use at most 128 MiB of HBM per device.

v0:
```python
import math

import jax
import jax.numpy as jnp
from jax import lax
from jax.sharding import PartitionSpec as P

DH = 64


eps = 1e-05


def layer_norm_forward(values, norm_gain_vector):
    full = values.astype(jnp.float32)
    centered_values = full - jnp.mean(full, axis=-1, keepdims=True)
    inverse_deviation = lax.rsqrt(
        jnp.mean(centered_values * centered_values, axis=-1, keepdims=True) + eps
    )
    standardized_input = centered_values * inverse_deviation
    return (
        (standardized_input * norm_gain_vector).astype(jnp.bfloat16),
        standardized_input,
        inverse_deviation,
    )


def layer_norm_backward(
    normalized_gradient, standardized_input, inverse_deviation, norm_gain_vector
):
    gain_scaled_gradient = normalized_gradient * norm_gain_vector
    first_moment_term = jnp.mean(gain_scaled_gradient, axis=-1, keepdims=True)
    second_moment_term = jnp.mean(gain_scaled_gradient * standardized_input, axis=-1, keepdims=True)
    return inverse_deviation * (
        gain_scaled_gradient - first_moment_term - standardized_input * second_moment_term
    )


def gelu_slope(hpre):
    return 0.5 * (1.0 + jax.scipy.special.erf(hpre / math.sqrt(2.0))) + hpre * jnp.exp(
        -0.5 * hpre * hpre
    ) / math.sqrt(2.0 * math.pi)


def softmax_rows(scores):
    top = jnp.max(scores, axis=-1, keepdims=True)
    expo = jnp.exp(scores - top)
    return expo / jnp.sum(expo, axis=-1, keepdims=True)


def softmax_back(probs, dprobs, scale):
    inner = jnp.sum(probs * dprobs, axis=-1, keepdims=True)
    return (probs * (dprobs - inner) * scale).astype(jnp.bfloat16)


def column_attend(pieces):
    queries, key_vecs, val_vecs, out_grad = pieces
    head_dim = queries.shape[3]
    scale = 1.0 / math.sqrt(head_dim)
    scores = (
        jnp.einsum("rchd,schd->chrs", queries, key_vecs, preferred_element_type=jnp.float32) * scale
    )
    probs = softmax_rows(scores)
    prob_bf = probs.astype(jnp.bfloat16)
    attended = jnp.einsum(
        "chrs,schd->rchd", prob_bf, val_vecs, preferred_element_type=jnp.float32
    ).astype(jnp.bfloat16)
    dprobs = jnp.einsum("rchd,schd->chrs", out_grad, val_vecs, preferred_element_type=jnp.float32)
    dscore = softmax_back(probs, dprobs, scale)
    grad_q = jnp.einsum(
        "chrs,schd->rchd", dscore, key_vecs, preferred_element_type=jnp.float32
    ).astype(jnp.bfloat16)
    grad_k = jnp.einsum(
        "chrs,rchd->schd", dscore, queries, preferred_element_type=jnp.float32
    ).astype(jnp.bfloat16)
    grad_v = jnp.einsum(
        "chrs,rchd->schd", prob_bf, out_grad, preferred_element_type=jnp.float32
    ).astype(jnp.bfloat16)
    return (attended, grad_q, grad_k, grad_v)


def contract_rows(left, right):
    return lax.dot_general(
        left, right, (((0,), (0,)), ((), ())), preferred_element_type=jnp.float32
    )


def contract_cols(left, right):
    return lax.dot_general(
        left, right, (((1,), (1,)), ((), ())), preferred_element_type=jnp.float32
    )


def initial_gradient(gradient_branch):
    full = gradient_branch.astype(jnp.float32)
    return full


def residual_norm_backward(
    base_gradient, running_partial_sum, standardized_input, inverse_deviation, norm_gain_vector
):
    normalized_gradient = lax.psum(running_partial_sum.astype(jnp.bfloat16), "heads").astype(
        jnp.float32
    )
    updated_gradient = base_gradient + layer_norm_backward(
        normalized_gradient, standardized_input, inverse_deviation, norm_gain_vector
    )
    return (updated_gradient, updated_gradient.astype(jnp.bfloat16))


def tied_whole(running_partial_sum):
    return lax.psum(running_partial_sum, "rows")


def weight_rows(normed, grads_flat):
    return lax.psum_scatter(
        contract_rows(normed, grads_flat), "rows", scatter_dimension=0, tiled=True
    )


def settle(pairs, early, normed, grads_flat):
    pairs.append((normed, grads_flat))
    early.append(weight_rows(normed, grads_flat))


def per_device(
    row_layer_input,
    column_layer_input,
    feedforward_layer_input,
    grad_out,
    layer_norm_gains,
    row_qkv,
    row_out,
    col_qkv,
    col_out,
    ffn_up,
    ffn_down,
):
    rows_dev, cols, feature_width = row_layer_input.shape
    token_positions = rows_dev * cols
    pairs = []
    early = []
    gradient_branch = grad_out.reshape(token_positions, feature_width)
    feedforward_normalized, standardized_feedforward_input, inverse_deviation_two = (
        layer_norm_forward(
            feedforward_layer_input.reshape(token_positions, feature_width), layer_norm_gains[2]
        )
    )
    hpre = jnp.dot(feedforward_normalized, ffn_up, preferred_element_type=jnp.float32)
    act_bf = jax.nn.gelu(hpre, approximate=False).astype(jnp.bfloat16)
    dact = jnp.dot(gradient_branch, ffn_down, preferred_element_type=jnp.float32)
    dpre = (dact * gelu_slope(hpre)).astype(jnp.bfloat16)
    norm_grad_two_piece = contract_cols(dpre, ffn_up)
    settle(pairs, early, feedforward_normalized, dpre)
    settle(pairs, early, gradient_branch, act_bf)
    feedforward_input_gradient, feedforward_gradient_branch = residual_norm_backward(
        initial_gradient(gradient_branch),
        norm_grad_two_piece,
        standardized_feedforward_input,
        inverse_deviation_two,
        layer_norm_gains[2],
    )
    column_normalized, standardized_column_input, inverse_deviation_one = layer_norm_forward(
        column_layer_input.reshape(token_positions, feature_width), layer_norm_gains[1]
    )
    col_flat = col_qkv.reshape(feature_width, -1)
    local = col_flat.shape[1] // 3
    heads = local // DH
    qkv = jnp.dot(column_normalized, col_flat, preferred_element_type=jnp.float32).astype(
        jnp.bfloat16
    )
    col_grad_o = jnp.dot(
        feedforward_gradient_branch, col_out, preferred_element_type=jnp.float32
    ).astype(jnp.bfloat16)
    sent = tuple(
        (
            item.reshape(rows_dev, cols, heads, DH)
            for item in (qkv[:, :local], qkv[:, local : 2 * local], qkv[:, 2 * local :], col_grad_o)
        )
    )
    in_columns = column_attend(
        (
            lax.all_to_all(sent[0], "rows", split_axis=1, concat_axis=0, tiled=True),
            lax.all_to_all(sent[1], "rows", split_axis=1, concat_axis=0, tiled=True),
            lax.all_to_all(sent[2], "rows", split_axis=1, concat_axis=0, tiled=True),
            lax.all_to_all(sent[3], "rows", split_axis=1, concat_axis=0, tiled=True),
        )
    )
    back = (
        lax.all_to_all(in_columns[0], "rows", split_axis=0, concat_axis=1, tiled=True),
        lax.all_to_all(in_columns[1], "rows", split_axis=0, concat_axis=1, tiled=True),
        lax.all_to_all(in_columns[2], "rows", split_axis=0, concat_axis=1, tiled=True),
        lax.all_to_all(in_columns[3], "rows", split_axis=0, concat_axis=1, tiled=True),
    )
    col_att, col_dq, col_dk, col_dv = [item.reshape(token_positions, local) for item in back]
    col_dqkv = jnp.concatenate([col_dq, col_dk, col_dv], axis=1)
    norm_grad_one_piece = contract_cols(col_dqkv, col_flat)
    settle(pairs, early, column_normalized, col_dqkv)
    settle(pairs, early, feedforward_gradient_branch, col_att)
    column_input_gradient, column_gradient_branch = residual_norm_backward(
        feedforward_input_gradient,
        norm_grad_one_piece,
        standardized_column_input,
        inverse_deviation_one,
        layer_norm_gains[1],
    )
    row_normalized, standardized_row_input, inverse_deviation_zero = layer_norm_forward(
        row_layer_input.reshape(token_positions, feature_width), layer_norm_gains[0]
    )
    row_flat = row_qkv.reshape(feature_width, -1)
    qkv = jnp.dot(row_normalized, row_flat, preferred_element_type=jnp.float32).astype(jnp.bfloat16)
    queries = qkv[:, :local].reshape(rows_dev, cols, heads, DH)
    key_vecs = qkv[:, local : 2 * local].reshape(rows_dev, cols, heads, DH)
    val_vecs = qkv[:, 2 * local :].reshape(rows_dev, cols, heads, DH)
    row_scale = 1.0 / math.sqrt(DH * rows_dev * lax.axis_size("rows"))
    logit_part = (
        jnp.einsum("sihd,sjhd->hij", queries, key_vecs, preferred_element_type=jnp.float32)
        * row_scale
    )
    out_grad = (
        jnp.dot(column_gradient_branch, row_out, preferred_element_type=jnp.float32)
        .astype(jnp.bfloat16)
        .reshape(rows_dev, cols, heads, DH)
    )
    dprob_part = jnp.einsum(
        "sihd,sjhd->hij", out_grad, val_vecs, preferred_element_type=jnp.float32
    )
    probs = softmax_rows(tied_whole(logit_part))
    prob_bf = probs.astype(jnp.bfloat16)
    dlogit = softmax_back(probs, tied_whole(dprob_part), row_scale)
    row_att = (
        jnp.einsum("hij,sjhd->sihd", prob_bf, val_vecs, preferred_element_type=jnp.float32)
        .astype(jnp.bfloat16)
        .reshape(token_positions, local)
    )
    grad_q = (
        jnp.einsum("hij,sjhd->sihd", dlogit, key_vecs, preferred_element_type=jnp.float32)
        .astype(jnp.bfloat16)
        .reshape(token_positions, local)
    )
    grad_k = (
        jnp.einsum("hij,sihd->sjhd", dlogit, queries, preferred_element_type=jnp.float32)
        .astype(jnp.bfloat16)
        .reshape(token_positions, local)
    )
    grad_v = (
        jnp.einsum("hij,sihd->sjhd", prob_bf, out_grad, preferred_element_type=jnp.float32)
        .astype(jnp.bfloat16)
        .reshape(token_positions, local)
    )
    row_dqkv = jnp.concatenate([grad_q, grad_k, grad_v], axis=1)
    norm_grad_zero_piece = contract_cols(row_dqkv, row_flat)
    settle(pairs, early, row_normalized, row_dqkv)
    settle(pairs, early, column_gradient_branch, row_att)
    closing_gradient, input_gradient_branch = residual_norm_backward(
        column_input_gradient,
        norm_grad_zero_piece,
        standardized_row_input,
        inverse_deviation_zero,
        layer_norm_gains[0],
    )
    input_gradient = input_gradient_branch.reshape(rows_dev, cols, feature_width)
    g_ffn_up, g_ffn_down, g_col_qkv, g_col_out, g_row_qkv, g_row_out = early
    share_rows = g_row_qkv.shape[0]
    return (
        input_gradient,
        g_row_qkv.reshape(share_rows, 3, local),
        g_row_out,
        g_col_qkv.reshape(share_rows, 3, local),
        g_col_out,
        g_ffn_up,
        g_ffn_down,
    )


def solution(mesh):
    return jax.shard_map(
        per_device,
        mesh=mesh,
        in_specs=(
            P("rows", None, None),
            P("rows", None, None),
            P("rows", None, None),
            P("rows", None, None),
            P(),
            P(None, None, "heads"),
            P(None, "heads"),
            P(None, None, "heads"),
            P(None, "heads"),
            P(None, "heads"),
            P(None, "heads"),
        ),
        out_specs=(
            P("rows", None, None),
            P("rows", None, "heads"),
            P("rows", "heads"),
            P("rows", None, "heads"),
            P("rows", "heads"),
            P("rows", "heads"),
            P("rows", "heads"),
        ),
        check_vma=False,
    )
```

profile of v0, /device:TPU:32, one launch (start us, length us, event | category | flops | bytes accessed | tf_op | source)
XLA Modules:
  0.0 794.3 jit_solution(692129298139085194)
XLA Ops:
  16.1 11.8 %all-to-all-start.1 = ((bf16[64,2,384]{2,1,0:T(2,128)(2,1)}), bf16[64,2,384]{2,1,0:T(2,128)(2,1)S(1)}, u32[]{:S(2)}, u32[]{:S(2)}) async-start(bf16[64,2,384]{2,1,0:T(2,128)(2,1)} %reshape.365), calls=%async_computation.1 | async-start | bytes 196608 | tf_op jit(solution)/shard_map/all_to_all | solution.py:183
  37.4 8.6 %all-to-all-start.3 = ((bf16[64,2,384]{2,1,0:T(2,128)(2,1)}), bf16[64,2,384]{2,1,0:T(2,128)(2,1)S(1)}, u32[]{:S(2)}, u32[]{:S(2)}) async-start(bf16[64,2,384]{2,1,0:T(2,128)(2,1)} %reshape.363), calls=%async_computation.3 | async-start | bytes 196608 | tf_op jit(solution)/shard_map/all_to_all | solution.py:185
  47.0 8.5 %all-to-all-done.3 = bf16[64,2,384]{2,1,0:T(2,128)(2,1)S(1)} async-done(((bf16[64,2,384]{2,1,0:T(2,128)(2,1)}), bf16[64,2,384]{2,1,0:T(2,128)(2,1)S(1)}, u32[]{:S(2)}, u32[]{:S(2)}) %all-to-all-start.3) | async-done | bytes 98336 | tf_op jit(solution)/shard_map/all_to_all | solution.py:185
  55.6 5.5 all-to-all-start
  61.4 9.3 %all-to-all-done = bf16[64,2,384]{2,1,0:T(2,128)(2,1)S(1)} async-done(((bf16[64,2,384]{2,1,0:T(2,128)(2,1)}), bf16[64,2,384]{2,1,0:T(2,128)(2,1)S(1)}, u32[]{:S(2)}, u32[]{:S(2)}) %all-to-all-start) | async-done | bytes 98336 | tf_op jit(solution)/shard_map/all_to_all | solution.py:184
  71.7 10.2 %all-reduce.18.cloned.1.call-done = bf16[256,768]{1,0:T(8,128)(2,1)} async-done(((bf16[256,768]{1,0:T(8,128)(2,1)}), bf16[256,768]{1,0:T(8,128)(2,1)}) %all-reduce.18.cloned.1.call-update) | async-done | bytes 393232 | tf_op jit(solution)/shard_map/psum | solution.py:102
  87.3 10.9 %all-to-all-start.2 = ((bf16[64,2,384]{2,1,0:T(2,128)(2,1)}), bf16[64,2,384]{2,1,0:T(2,128)(2,1)S(1)}, u32[]{:S(2)}, u32[]{:S(2)}) async-start(bf16[64,2,384]{2,1,0:T(2,128)(2,1)} %reshape.361), calls=%async_computation.2 | async-start | bytes 196608 | tf_op jit(solution)/shard_map/all_to_all | solution.py:186
  98.2 2.8 fusion.158
  101.0 6.6 all-to-all-done.2
  109.1 2.3 fusion.23
  112.5 5.5 all-to-all-start.4
  119.3 2.9 fusion.24
  124.2 3.5 all-to-all-done.4
  127.7 6.8 all-to-all-start.5
  137.0 7.1 all-to-all-done.5
  144.1 6.2 all-to-all-start.6
  155.1 4.9 all-to-all-done.6
  161.5 2.5 convolution_convert_fusion.1
  169.3 37.9 %all-reduce.20.cloned.1.call-done = bf16[256,768]{1,0:T(8,128)(2,1)} async-done(((bf16[256,768]{1,0:T(8,128)(2,1)}), bf16[256,768]{1,0:T(8,128)(2,1)}) %all-reduce.20.cloned.1.call-update) | async-done | bytes 393232 | tf_op jit(solution)/shard_map/psum | solution.py:102
  208.5 2.1 multiply_convert_fusion
  214.7 176.8 %all-reduce.24.cloned.1.call-done = (f32[3,64,64]{2,1,0:T(8,128)}, f32[3,64,64]{2,1,0:T(8,128)}) async-done(((f32[3,64,64]{2,1,0:T(8,128)}, f32[3,64,64]{2,1,0:T(8,128)}), (f32[3,64,64]{2,1,0:T(8,128)}, f32[3,64,64]{2,1,0:T(8,128)})) %all-reduce.24.cloned.1.call-update) | async-done | bytes 98320 | tf_op jit(solution)/shard_map/psum | solution.py:112
  392.7 2.5 fusion.15
  395.2 2.3 fusion.14
  397.5 2.1 fusion.16
  406.5 2.5 convolution_convert_fusion
  409.0 9.6 %all-reduce.26.cloned.1.call-start = ((), (), s32[]{:S(2)}) async-start(), calls=%async_computation.12 | async-start | bytes 12582912
  418.7 4.8 convolution_bitcast_fusion
  423.6 3.0 fusion.163
  426.6 30.9 %all-reduce.22.cloned.1.call-done = bf16[256,768]{1,0:T(8,128)(2,1)} async-done(((bf16[256,768]{1,0:T(8,128)(2,1)}), bf16[256,768]{1,0:T(8,128)(2,1)}) %all-reduce.22.cloned.1.call-update) | async-done | bytes 393232 | tf_op jit(solution)/shard_map/psum | solution.py:102
  458.8 2.1 multiply_convert_fusion.1
  463.4 2.2 fusion.26
  469.1 10.7 %all-to-all-start.7 = ((bf16[64,2,384]{2,1,0:T(2,128)(2,1)}), bf16[64,2,384]{2,1,0:T(2,128)(2,1)}, u32[]{:S(2)}, u32[]{:S(2)}) async-start(bf16[64,2,384]{2,1,0:T(2,128)(2,1)} %reshape.373), calls=%async_computation.7 | async-start | bytes 196608 | tf_op jit(solution)/shard_map/all_to_all | solution.py:190
  481.7 7.6 all-to-all-done.7
  496.3 133.9 %fusion.154 = (f32[16,192]{1,0:T(8,128)S(1)}, f32[16,192]{1,0:T(8,128)S(1)}, f32[16,768]{1,0:T(8,128)S(1)}) fusion(f32[768,192]{1,0:T(8,128)S(1)} %fusion.88, f32[768,192]{1,0:T(8,128)S(1)} %fusion.93, f32[768,768]{1,0:T(8,128)} %fusion.164), kind=kCustom, calls=%all-reduce-scatter.3 | all-reduce-scatter fusion | flops 1179649 | bytes 3613696
  631.6 10.7 %collective-permute-start.13 = (f32[16,192]{1,0:T(8,128)S(1)}, f32[16,192]{1,0:T(8,128)S(1)}, u32[]{:S(2)}, u32[]{:S(2)}) collective-permute-start(f32[16,192]{1,0:T(8,128)S(1)} %get-tuple-element.45), channel_id=1, source_target_pairs={{0,56},{4,60},{8,64},{12,68},{16,72},{20,76},{24,80},{28,84},{32,8... | collective-permute-start | bytes 36872
  642.2 8.1 %collective-permute-start.12 = (f32[16,192]{1,0:T(8,128)S(1)}, f32[16,192]{1,0:T(8,128)S(1)}, u32[]{:S(2)}, u32[]{:S(2)}) collective-permute-start(f32[16,192]{1,0:T(8,128)S(1)} %get-tuple-element.45), channel_id=1, source_target_pairs={{0,52},{4,56},{8,60},{12,64},{16,68},{20,72},{24,76},{28,80},{32,8... | collective-permute-start | bytes 36872
  653.1 17.0 %collective-permute-start.11 = (f32[16,192]{1,0:T(8,128)S(1)}, f32[16,192]{1,0:T(8,128)S(1)}, u32[]{:S(2)}, u32[]{:S(2)}) collective-permute-start(f32[16,192]{1,0:T(8,128)S(1)} %get-tuple-element.45), channel_id=1, source_target_pairs={{0,48},{4,52},{8,56},{12,60},{16,64},{20,68},{24,72},{28,76},{32,8... | collective-permute-start | bytes 36872
  671.4 3.1 collective-permute-start.9
  674.5 4.3 collective-permute-start.8
  680.7 3.7 collective-permute-start.6
  684.5 2.2 collective-permute-start.5
  688.7 3.7 collective-permute-start.3
  694.3 2.1 collective-permute-start.1
  696.4 3.2 collective-permute-start
  701.6 2.3 collective-permute-start.29
  703.9 2.7 collective-permute-start.28
  714.2 2.8 collective-permute-start.23
  717.1 2.5 collective-permute-start.22
  719.6 3.1 collective-permute-start.21
  724.7 3.4 collective-permute-start.19
  730.0 2.0 collective-permute-start.17
  732.0 3.4 collective-permute-start.16
  737.0 2.3 collective-permute-start.45
  739.3 2.4 collective-permute-start.44
  751.7 2.2 collective-permute-start.39
  753.9 3.5 collective-permute-start.38
  757.5 2.1 collective-permute-start.37
  762.0 2.1 collective-permute-start.36
  764.1 3.6 collective-permute-start.35
  769.6 2.0 collective-permute-start.33
  771.6 3.1 collective-permute-start.32
  775.6 2.4 collective-permute-done.33
  778.0 2.0 collective-permute-done.32
  780.0 2.0 concatenate.10
  (278 shorter events, 120.7 us)
Async XLA Ops:
  16.1 21.3 %all-to-all-start.1 = ((bf16[64,2,384]{2,1,0:T(2,128)(2,1)}), bf16[64,2,384]{2,1,0:T(2,128)(2,1)S(1)}, u32[]{:S(2)}, u32[]{:S(2)}) async-start(bf16[64,2,384]{2,1,0:T(2,128)(2,1)} %reshape.365), calls=%async_computation.1 | async-start | bytes 196608 | tf_op jit(solution)/shard_map/all_to_all | solution.py:183
  27.9 54.1 %all-reduce.18.cloned.1.call-start = ((), (), s32[]{:S(2)}) async-start(), calls=%async_computation.8 | async-start | bytes 786432 | tf_op jit(solution)/shard_map/psum | solution.py:102
  34.9 47.1 %copy-start.25 = (f32[256]{0:T(256)S(1)}, f32[256]{0:T(256)}, u32[]{:S(2)}) copy-start(f32[256]{0:T(256)} %copy-done.24) | copy-start | bytes 3076
  37.4 18.2 %all-to-all-start.3 = ((bf16[64,2,384]{2,1,0:T(2,128)(2,1)}), bf16[64,2,384]{2,1,0:T(2,128)(2,1)S(1)}, u32[]{:S(2)}, u32[]{:S(2)}) async-start(bf16[64,2,384]{2,1,0:T(2,128)(2,1)} %reshape.363), calls=%async_computation.3 | async-start | bytes 196608 | tf_op jit(solution)/shard_map/all_to_all | solution.py:185
  55.6 15.1 %all-to-all-start = ((bf16[64,2,384]{2,1,0:T(2,128)(2,1)}), bf16[64,2,384]{2,1,0:T(2,128)(2,1)S(1)}, u32[]{:S(2)}, u32[]{:S(2)}) async-start(bf16[64,2,384]{2,1,0:T(2,128)(2,1)} %reshape.359), calls=%async_computation | async-start | bytes 196608 | tf_op jit(solution)/shard_map/all_to_all | solution.py:184
  87.3 20.3 %all-to-all-start.2 = ((bf16[64,2,384]{2,1,0:T(2,128)(2,1)}), bf16[64,2,384]{2,1,0:T(2,128)(2,1)S(1)}, u32[]{:S(2)}, u32[]{:S(2)}) async-start(bf16[64,2,384]{2,1,0:T(2,128)(2,1)} %reshape.361), calls=%async_computation.2 | async-start | bytes 196608 | tf_op jit(solution)/shard_map/all_to_all | solution.py:186
  112.5 15.2 %all-to-all-start.4 = ((bf16[64,2,384]{2,1,0:T(2,128)(2,1)}), bf16[64,2,384]{2,1,0:T(2,128)(2,1)S(1)}, u32[]{:S(2)}, u32[]{:S(2)}) async-start(bf16[64,2,384]{2,1,0:T(2,128)(2,1)} %reshape.367), calls=%async_computation.4 | async-start | bytes 196608 | tf_op jit(solution)/shard_map/all_to_all | solution.py:191
  127.7 16.4 %all-to-all-start.5 = ((bf16[64,2,384]{2,1,0:T(2,128)(2,1)}), bf16[64,2,384]{2,1,0:T(2,128)(2,1)S(1)}, u32[]{:S(2)}, u32[]{:S(2)}) async-start(bf16[64,2,384]{2,1,0:T(2,128)(2,1)} %reshape.369), calls=%async_computation.5 | async-start | bytes 196608 | tf_op jit(solution)/shard_map/all_to_all | solution.py:192
  144.1 15.8 %all-to-all-start.6 = ((bf16[64,2,384]{2,1,0:T(2,128)(2,1)}), bf16[64,2,384]{2,1,0:T(2,128)(2,1)}, u32[]{:S(2)}, u32[]{:S(2)}) async-start(bf16[64,2,384]{2,1,0:T(2,128)(2,1)} %reshape.371), calls=%async_computation.6 | async-start | bytes 196608 | tf_op jit(solution)/shard_map/all_to_all | solution.py:193
  150.3 56.8 %all-reduce.20.cloned.1.call-start = ((), (), s32[]{:S(2)}) async-start(), calls=%async_computation.9 | async-start | bytes 786432 | tf_op jit(solution)/shard_map/psum | solution.py:102
  164.1 227.5 %all-reduce.24.cloned.1.call-start = ((), (), s32[]{:S(2)}) async-start(), calls=%async_computation.11 | async-start | bytes 393216 | tf_op jit(solution)/shard_map/psum | solution.py:112
  210.6 184.5 %copy-start.17 = (bf16[4,64,3,64]{1,0,3,2:T(4,128)(2,1)S(1)}, bf16[4,64,3,64]{1,0,3,2:T(4,128)(2,1)}, u32[]{:S(2)}) copy-start(bf16[4,64,3,64]{1,0,3,2:T(4,128)(2,1)} %copy-done.16) | copy-start | bytes 294916
  214.7 242.8 %all-reduce.22.cloned.1.call-start = ((), (), s32[]{:S(2)}) async-start(), calls=%async_computation.10 | async-start | bytes 786432 | tf_op jit(solution)/shard_map/psum | solution.py:102
  409.0 373.6 %all-reduce.26.cloned.1.call-start = ((), (), s32[]{:S(2)}) async-start(), calls=%async_computation.12 | async-start | bytes 12582912
  469.1 20.2 %all-to-all-start.7 = ((bf16[64,2,384]{2,1,0:T(2,128)(2,1)}), bf16[64,2,384]{2,1,0:T(2,128)(2,1)}, u32[]{:S(2)}, u32[]{:S(2)}) async-start(bf16[64,2,384]{2,1,0:T(2,128)(2,1)} %reshape.373), calls=%async_computation.7 | async-start | bytes 196608 | tf_op jit(solution)/shard_map/all_to_all | solution.py:190
  496.3 248.4 %copy-start.31 = (u32[256]{0:T(256)S(1)}, u32[256]{0:T(256)}, u32[]{:S(2)}) copy-start(u32[256]{0:T(256)} %constant.96) | copy-start | bytes 3076
  630.3 41.1 %collective-permute-start.14 = (f32[16,192]{1,0:T(8,128)S(1)}, f32[16,192]{1,0:T(8,128)S(1)}, u32[]{:S(2)}, u32[]{:S(2)}) collective-permute-start(f32[16,192]{1,0:T(8,128)S(1)} %get-tuple-element.45), channel_id=1, source_target_pairs={{0,60},{4,64},{8,68},{12,72},{16,76},{20,80},{24,84},{28,88},{32,9... | collective-permute-start | bytes 36872
  631.6 42.9 %collective-permute-start.13 = (f32[16,192]{1,0:T(8,128)S(1)}, f32[16,192]{1,0:T(8,128)S(1)}, u32[]{:S(2)}, u32[]{:S(2)}) collective-permute-start(f32[16,192]{1,0:T(8,128)S(1)} %get-tuple-element.45), channel_id=1, source_target_pairs={{0,56},{4,60},{8,64},{12,68},{16,72},{20,76},{24,80},{28,84},{32,8... | collective-permute-start | bytes 36872
  642.2 36.6 %collective-permute-start.12 = (f32[16,192]{1,0:T(8,128)S(1)}, f32[16,192]{1,0:T(8,128)S(1)}, u32[]{:S(2)}, u32[]{:S(2)}) collective-permute-start(f32[16,192]{1,0:T(8,128)S(1)} %get-tuple-element.45), channel_id=1, source_target_pairs={{0,52},{4,56},{8,60},{12,64},{16,68},{20,72},{24,76},{28,80},{32,8... | collective-permute-start | bytes 36872
  650.4 2.7 collective-permute-start.31
  651.7 18.4 %collective-permute-start.15 = (f32[12,192]{1,0:T(8,128)S(1)}, f32[12,192]{1,0:T(8,128)S(1)}, u32[]{:S(2)}, u32[]{:S(2)}) collective-permute-start(f32[12,192]{1,0:T(8,128)S(1)} %slice.45), channel_id=1, source_target_pairs={{0,64},{4,68},{8,72},{12,76},{16,80},{20,84},{24,88},{28,92},{32,9... | collective-permute-start | bytes 27656
  653.1 27.7 %collective-permute-start.11 = (f32[16,192]{1,0:T(8,128)S(1)}, f32[16,192]{1,0:T(8,128)S(1)}, u32[]{:S(2)}, u32[]{:S(2)}) collective-permute-start(f32[16,192]{1,0:T(8,128)S(1)} %get-tuple-element.45), channel_id=1, source_target_pairs={{0,48},{4,52},{8,56},{12,60},{16,64},{20,68},{24,72},{28,76},{32,8... | collective-permute-start | bytes 36872
  670.1 14.4 %collective-permute-start.10 = (f32[16,192]{1,0:T(8,128)S(1)}, f32[16,192]{1,0:T(8,128)S(1)}, u32[]{:S(2)}, u32[]{:S(2)}) collective-permute-start(f32[16,192]{1,0:T(8,128)S(1)} %get-tuple-element.45), channel_id=1, source_target_pairs={{0,44},{4,48},{8,52},{12,56},{16,60},{20,64},{24,68},{28,72},{32,7... | collective-permute-start | bytes 36872
  671.4 15.3 %collective-permute-start.9 = (f32[16,192]{1,0:T(8,128)S(1)}, f32[16,192]{1,0:T(8,128)S(1)}, u32[]{:S(2)}, u32[]{:S(2)}) collective-permute-start(f32[16,192]{1,0:T(8,128)S(1)} %get-tuple-element.45), channel_id=1, source_target_pairs={{0,40},{4,44},{8,48},{12,52},{16,56},{20,60},{24,64},{28,68},{32,7... | collective-permute-start | bytes 36872
  674.5 14.2 %collective-permute-start.8 = (f32[16,192]{1,0:T(8,128)S(1)}, f32[16,192]{1,0:T(8,128)S(1)}, u32[]{:S(2)}, u32[]{:S(2)}) collective-permute-start(f32[16,192]{1,0:T(8,128)S(1)} %get-tuple-element.45), channel_id=1, source_target_pairs={{0,36},{4,40},{8,44},{12,48},{16,52},{20,56},{24,60},{28,64},{32,6... | collective-permute-start | bytes 36872
  678.8 13.6 %collective-permute-start.7 = (f32[16,192]{1,0:T(8,128)S(1)}, f32[16,192]{1,0:T(8,128)S(1)}, u32[]{:S(2)}, u32[]{:S(2)}) collective-permute-start(f32[16,192]{1,0:T(8,128)S(1)} %get-tuple-element.45), channel_id=1, source_target_pairs={{0,32},{4,36},{8,40},{12,44},{16,48},{20,52},{24,56},{28,60},{32,6... | collective-permute-start | bytes 36872
  680.7 13.6 %collective-permute-start.6 = (f32[16,192]{1,0:T(8,128)S(1)}, f32[16,192]{1,0:T(8,128)S(1)}, u32[]{:S(2)}, u32[]{:S(2)}) collective-permute-start(f32[16,192]{1,0:T(8,128)S(1)} %get-tuple-element.45), channel_id=1, source_target_pairs={{0,28},{4,32},{8,36},{12,40},{16,44},{20,48},{24,52},{28,56},{32,6... | collective-permute-start | bytes 36872
  684.5 11.9 %collective-permute-start.5 = (f32[16,192]{1,0:T(8,128)S(1)}, f32[16,192]{1,0:T(8,128)S(1)}, u32[]{:S(2)}, u32[]{:S(2)}) collective-permute-start(f32[16,192]{1,0:T(8,128)S(1)} %get-tuple-element.45), channel_id=1, source_target_pairs={{0,24},{4,28},{8,32},{12,36},{16,40},{20,44},{24,48},{28,52},{32,5... | collective-permute-start | bytes 36872
  686.7 13.0 %collective-permute-start.4 = (f32[16,192]{1,0:T(8,128)S(1)}, f32[16,192]{1,0:T(8,128)S(1)}, u32[]{:S(2)}, u32[]{:S(2)}) collective-permute-start(f32[16,192]{1,0:T(8,128)S(1)} %get-tuple-element.45), channel_id=1, source_target_pairs={{0,20},{4,24},{8,28},{12,32},{16,36},{20,40},{24,44},{28,48},{32,5... | collective-permute-start | bytes 36872
  688.7 12.9 %collective-permute-start.3 = (f32[16,192]{1,0:T(8,128)S(1)}, f32[16,192]{1,0:T(8,128)S(1)}, u32[]{:S(2)}, u32[]{:S(2)}) collective-permute-start(f32[16,192]{1,0:T(8,128)S(1)} %get-tuple-element.45), channel_id=1, source_target_pairs={{0,16},{4,20},{8,24},{12,28},{16,32},{20,36},{24,40},{28,44},{32,4... | collective-permute-start | bytes 36872
  692.4 11.5 %collective-permute-start.2 = (f32[16,192]{1,0:T(8,128)S(1)}, f32[16,192]{1,0:T(8,128)S(1)}, u32[]{:S(2)}, u32[]{:S(2)}) collective-permute-start(f32[16,192]{1,0:T(8,128)S(1)} %get-tuple-element.45), channel_id=1, source_target_pairs={{0,12},{4,16},{8,20},{12,24},{16,28},{20,32},{24,36},{28,40},{32,4... | collective-permute-start | bytes 36872
  694.3 12.3 %collective-permute-start.1 = (f32[16,192]{1,0:T(8,128)S(1)}, f32[16,192]{1,0:T(8,128)S(1)}, u32[]{:S(2)}, u32[]{:S(2)}) collective-permute-start(f32[16,192]{1,0:T(8,128)S(1)} %get-tuple-element.45), channel_id=1, source_target_pairs={{0,8},{4,12},{8,16},{12,20},{16,24},{20,28},{24,32},{28,36},{32,40... | collective-permute-start | bytes 36872
  696.4 11.6 %collective-permute-start = (f32[16,192]{1,0:T(8,128)S(1)}, f32[16,192]{1,0:T(8,128)S(1)}, u32[]{:S(2)}, u32[]{:S(2)}) collective-permute-start(f32[16,192]{1,0:T(8,128)S(1)} %get-tuple-element.45), channel_id=1, source_target_pairs={{0,4},{4,8},{8,12},{12,16},{16,20},{20,24},{24,28},{28,32},{32,36}... | collective-permute-start | bytes 36872
  699.7 9.7 %collective-permute-start.30 = (f32[16,192]{1,0:T(8,128)S(1)}, f32[16,192]{1,0:T(8,128)S(1)}, u32[]{:S(2)}, u32[]{:S(2)}) collective-permute-start(f32[16,192]{1,0:T(8,128)S(1)} %get-tuple-element.46), channel_id=1, source_target_pairs={{0,60},{4,64},{8,68},{12,72},{16,76},{20,80},{24,84},{28,88},{32,9... | collective-permute-start | bytes 36872
  701.6 9.8 %collective-permute-start.29 = (f32[16,192]{1,0:T(8,128)S(1)}, f32[16,192]{1,0:T(8,128)S(1)}, u32[]{:S(2)}, u32[]{:S(2)}) collective-permute-start(f32[16,192]{1,0:T(8,128)S(1)} %get-tuple-element.46), channel_id=1, source_target_pairs={{0,56},{4,60},{8,64},{12,68},{16,72},{20,76},{24,80},{28,84},{32,8... | collective-permute-start | bytes 36872
  703.9 9.0 %collective-permute-start.28 = (f32[16,192]{1,0:T(8,128)S(1)}, f32[16,192]{1,0:T(8,128)S(1)}, u32[]{:S(2)}, u32[]{:S(2)}) collective-permute-start(f32[16,192]{1,0:T(8,128)S(1)} %get-tuple-element.46), channel_id=1, source_target_pairs={{0,52},{4,56},{8,60},{12,64},{16,68},{20,72},{24,76},{28,80},{32,8... | collective-permute-start | bytes 36872
  706.6 7.6 collective-permute-start.27
  708.1 9.0 %collective-permute-start.26 = (f32[16,192]{1,0:T(8,128)S(1)}, f32[16,192]{1,0:T(8,128)S(1)}, u32[]{:S(2)}, u32[]{:S(2)}) collective-permute-start(f32[16,192]{1,0:T(8,128)S(1)} %get-tuple-element.46), channel_id=1, source_target_pairs={{0,44},{4,48},{8,52},{12,56},{16,60},{20,64},{24,68},{28,72},{32,7... | collective-permute-start | bytes 36872
  709.4 10.2 %collective-permute-start.25 = (f32[16,192]{1,0:T(8,128)S(1)}, f32[16,192]{1,0:T(8,128)S(1)}, u32[]{:S(2)}, u32[]{:S(2)}) collective-permute-start(f32[16,192]{1,0:T(8,128)S(1)} %get-tuple-element.46), channel_id=1, source_target_pairs={{0,40},{4,44},{8,48},{12,52},{16,56},{20,60},{24,64},{28,68},{32,7... | collective-permute-start | bytes 36872
  711.3 11.4 %collective-permute-start.24 = (f32[16,192]{1,0:T(8,128)S(1)}, f32[16,192]{1,0:T(8,128)S(1)}, u32[]{:S(2)}, u32[]{:S(2)}) collective-permute-start(f32[16,192]{1,0:T(8,128)S(1)} %get-tuple-element.46), channel_id=1, source_target_pairs={{0,36},{4,40},{8,44},{12,48},{16,52},{20,56},{24,60},{28,64},{32,6... | collective-permute-start | bytes 36872
  712.9 30.5 %collective-permute-start.47 = (f32[12,768]{1,0:T(8,128)S(1)}, f32[12,768]{1,0:T(8,128)S(1)}, u32[]{:S(2)}, u32[]{:S(2)}) collective-permute-start(f32[12,768]{1,0:T(8,128)S(1)} %slice.47), channel_id=1, source_target_pairs={{0,64},{4,68},{8,72},{12,76},{16,80},{20,84},{24,88},{28,92},{32,9... | collective-permute-start | bytes 110600
  714.2 10.4 %collective-permute-start.23 = (f32[16,192]{1,0:T(8,128)S(1)}, f32[16,192]{1,0:T(8,128)S(1)}, u32[]{:S(2)}, u32[]{:S(2)}) collective-permute-start(f32[16,192]{1,0:T(8,128)S(1)} %get-tuple-element.46), channel_id=1, source_target_pairs={{0,32},{4,36},{8,40},{12,44},{16,48},{20,52},{24,56},{28,60},{32,6... | collective-permute-start | bytes 36872
  717.1 11.0 %collective-permute-start.22 = (f32[16,192]{1,0:T(8,128)S(1)}, f32[16,192]{1,0:T(8,128)S(1)}, u32[]{:S(2)}, u32[]{:S(2)}) collective-permute-start(f32[16,192]{1,0:T(8,128)S(1)} %get-tuple-element.46), channel_id=1, source_target_pairs={{0,28},{4,32},{8,36},{12,40},{16,44},{20,48},{24,52},{28,56},{32,6... | collective-permute-start | bytes 36872
  719.6 10.4 %collective-permute-start.21 = (f32[16,192]{1,0:T(8,128)S(1)}, f32[16,192]{1,0:T(8,128)S(1)}, u32[]{:S(2)}, u32[]{:S(2)}) collective-permute-start(f32[16,192]{1,0:T(8,128)S(1)} %get-tuple-element.46), channel_id=1, source_target_pairs={{0,24},{4,28},{8,32},{12,36},{16,40},{20,44},{24,48},{28,52},{32,5... | collective-permute-start | bytes 36872
  722.7 9.3 %collective-permute-start.20 = (f32[16,192]{1,0:T(8,128)S(1)}, f32[16,192]{1,0:T(8,128)S(1)}, u32[]{:S(2)}, u32[]{:S(2)}) collective-permute-start(f32[16,192]{1,0:T(8,128)S(1)} %get-tuple-element.46), channel_id=1, source_target_pairs={{0,20},{4,24},{8,28},{12,32},{16,36},{20,40},{24,44},{28,48},{32,5... | collective-permute-start | bytes 36872
  724.7 10.8 %collective-permute-start.19 = (f32[16,192]{1,0:T(8,128)S(1)}, f32[16,192]{1,0:T(8,128)S(1)}, u32[]{:S(2)}, u32[]{:S(2)}) collective-permute-start(f32[16,192]{1,0:T(8,128)S(1)} %get-tuple-element.46), channel_id=1, source_target_pairs={{0,16},{4,20},{8,24},{12,28},{16,32},{20,36},{24,40},{28,44},{32,4... | collective-permute-start | bytes 36872
  728.1 8.9 %collective-permute-start.18 = (f32[16,192]{1,0:T(8,128)S(1)}, f32[16,192]{1,0:T(8,128)S(1)}, u32[]{:S(2)}, u32[]{:S(2)}) collective-permute-start(f32[16,192]{1,0:T(8,128)S(1)} %get-tuple-element.46), channel_id=1, source_target_pairs={{0,12},{4,16},{8,20},{12,24},{16,28},{20,32},{24,36},{28,40},{32,4... | collective-permute-start | bytes 36872
  730.0 9.3 %collective-permute-start.17 = (f32[16,192]{1,0:T(8,128)S(1)}, f32[16,192]{1,0:T(8,128)S(1)}, u32[]{:S(2)}, u32[]{:S(2)}) collective-permute-start(f32[16,192]{1,0:T(8,128)S(1)} %get-tuple-element.46), channel_id=1, source_target_pairs={{0,8},{4,12},{8,16},{12,20},{16,24},{20,28},{24,32},{28,36},{32,40... | collective-permute-start | bytes 36872
  732.0 9.7 %collective-permute-start.16 = (f32[16,192]{1,0:T(8,128)S(1)}, f32[16,192]{1,0:T(8,128)S(1)}, u32[]{:S(2)}, u32[]{:S(2)}) collective-permute-start(f32[16,192]{1,0:T(8,128)S(1)} %get-tuple-element.46), channel_id=1, source_target_pairs={{0,4},{4,8},{8,12},{12,16},{16,20},{20,24},{24,28},{28,32},{32,36}... | collective-permute-start | bytes 36872
  735.5 13.1 %collective-permute-start.46 = (f32[16,768]{1,0:T(8,128)S(1)}, f32[16,768]{1,0:T(8,128)S(1)}, u32[]{:S(2)}, u32[]{:S(2)}) collective-permute-start(f32[16,768]{1,0:T(8,128)S(1)} %get-tuple-element.47), channel_id=1, source_target_pairs={{0,60},{4,64},{8,68},{12,72},{16,76},{20,80},{24,84},{28,88},{32,9... | collective-permute-start | bytes 147464
  737.0 13.2 %collective-permute-start.45 = (f32[16,768]{1,0:T(8,128)S(1)}, f32[16,768]{1,0:T(8,128)S(1)}, u32[]{:S(2)}, u32[]{:S(2)}) collective-permute-start(f32[16,768]{1,0:T(8,128)S(1)} %get-tuple-element.47), channel_id=1, source_target_pairs={{0,56},{4,60},{8,64},{12,68},{16,72},{20,76},{24,80},{28,84},{32,8... | collective-permute-start | bytes 147464
  739.3 12.4 %collective-permute-start.44 = (f32[16,768]{1,0:T(8,128)S(1)}, f32[16,768]{1,0:T(8,128)S(1)}, u32[]{:S(2)}, u32[]{:S(2)}) collective-permute-start(f32[16,768]{1,0:T(8,128)S(1)} %get-tuple-element.47), channel_id=1, source_target_pairs={{0,52},{4,56},{8,60},{12,64},{16,68},{20,72},{24,76},{28,80},{32,8... | collective-permute-start | bytes 147464
  741.7 12.2 %collective-permute-start.43 = (f32[16,768]{1,0:T(8,128)S(1)}, f32[16,768]{1,0:T(8,128)S(1)}, u32[]{:S(2)}, u32[]{:S(2)}) collective-permute-start(f32[16,768]{1,0:T(8,128)S(1)} %get-tuple-element.47), channel_id=1, source_target_pairs={{0,48},{4,52},{8,56},{12,60},{16,64},{20,68},{24,72},{28,76},{32,8... | collective-permute-start | bytes 147464
  743.5 14.0 %collective-permute-start.42 = (f32[16,768]{1,0:T(8,128)S(1)}, f32[16,768]{1,0:T(8,128)S(1)}, u32[]{:S(2)}, u32[]{:S(2)}) collective-permute-start(f32[16,768]{1,0:T(8,128)S(1)} %get-tuple-element.47), channel_id=1, source_target_pairs={{0,44},{4,48},{8,52},{12,56},{16,60},{20,64},{24,68},{28,72},{32,7... | collective-permute-start | bytes 147464
  748.5 13.5 %collective-permute-start.41 = (f32[16,768]{1,0:T(8,128)S(1)}, f32[16,768]{1,0:T(8,128)S(1)}, u32[]{:S(2)}, u32[]{:S(2)}) collective-permute-start(f32[16,768]{1,0:T(8,128)S(1)} %get-tuple-element.47), channel_id=1, source_target_pairs={{0,40},{4,44},{8,48},{12,52},{16,56},{20,60},{24,64},{28,68},{32,7... | collective-permute-start | bytes 147464
  750.2 13.9 %collective-permute-start.40 = (f32[16,768]{1,0:T(8,128)S(1)}, f32[16,768]{1,0:T(8,128)S(1)}, u32[]{:S(2)}, u32[]{:S(2)}) collective-permute-start(f32[16,768]{1,0:T(8,128)S(1)} %get-tuple-element.47), channel_id=1, source_target_pairs={{0,36},{4,40},{8,44},{12,48},{16,52},{20,56},{24,60},{28,64},{32,6... | collective-permute-start | bytes 147464
  751.7 16.0 %collective-permute-start.39 = (f32[16,768]{1,0:T(8,128)S(1)}, f32[16,768]{1,0:T(8,128)S(1)}, u32[]{:S(2)}, u32[]{:S(2)}) collective-permute-start(f32[16,768]{1,0:T(8,128)S(1)} %get-tuple-element.47), channel_id=1, source_target_pairs={{0,32},{4,36},{8,40},{12,44},{16,48},{20,52},{24,56},{28,60},{32,6... | collective-permute-start | bytes 147464
  753.9 15.7 %collective-permute-start.38 = (f32[16,768]{1,0:T(8,128)S(1)}, f32[16,768]{1,0:T(8,128)S(1)}, u32[]{:S(2)}, u32[]{:S(2)}) collective-permute-start(f32[16,768]{1,0:T(8,128)S(1)} %get-tuple-element.47), channel_id=1, source_target_pairs={{0,28},{4,32},{8,36},{12,40},{16,44},{20,48},{24,52},{28,56},{32,6... | collective-permute-start | bytes 147464
  757.5 14.2 %collective-permute-start.37 = (f32[16,768]{1,0:T(8,128)S(1)}, f32[16,768]{1,0:T(8,128)S(1)}, u32[]{:S(2)}, u32[]{:S(2)}) collective-permute-start(f32[16,768]{1,0:T(8,128)S(1)} %get-tuple-element.47), channel_id=1, source_target_pairs={{0,24},{4,28},{8,32},{12,36},{16,40},{20,44},{24,48},{28,52},{32,5... | collective-permute-start | bytes 147464
  762.0 13.4 %collective-permute-start.36 = (f32[16,768]{1,0:T(8,128)S(1)}, f32[16,768]{1,0:T(8,128)S(1)}, u32[]{:S(2)}, u32[]{:S(2)}) collective-permute-start(f32[16,768]{1,0:T(8,128)S(1)} %get-tuple-element.47), channel_id=1, source_target_pairs={{0,20},{4,24},{8,28},{12,32},{16,36},{20,40},{24,44},{28,48},{32,5... | collective-permute-start | bytes 147464
  764.1 11.3 %collective-permute-start.35 = (f32[16,768]{1,0:T(8,128)S(1)}, f32[16,768]{1,0:T(8,128)S(1)}, u32[]{:S(2)}, u32[]{:S(2)}) collective-permute-start(f32[16,768]{1,0:T(8,128)S(1)} %get-tuple-element.47), channel_id=1, source_target_pairs={{0,16},{4,20},{8,24},{12,28},{16,32},{20,36},{24,40},{28,44},{32,4... | collective-permute-start | bytes 147464
  767.7 7.9 collective-permute-start.34
  769.6 8.3 %collective-permute-start.33 = (f32[16,768]{1,0:T(8,128)S(1)}, f32[16,768]{1,0:T(8,128)S(1)}, u32[]{:S(2)}, u32[]{:S(2)}) collective-permute-start(f32[16,768]{1,0:T(8,128)S(1)} %get-tuple-element.47), channel_id=1, source_target_pairs={{0,8},{4,12},{8,16},{12,20},{16,24},{20,28},{24,32},{28,36},{32,40... | collective-permute-start | bytes 147464
  771.6 8.3 %collective-permute-start.32 = (f32[16,768]{1,0:T(8,128)S(1)}, f32[16,768]{1,0:T(8,128)S(1)}, u32[]{:S(2)}, u32[]{:S(2)}) collective-permute-start(f32[16,768]{1,0:T(8,128)S(1)} %get-tuple-element.47), channel_id=1, source_target_pairs={{0,4},{4,8},{8,12},{12,16},{16,20},{20,24},{24,28},{28,32},{32,36}... | collective-permute-start | bytes 147464
  (32 other events, 493.9 us)
Sparse Core Ops, SparseCore 0:
  33.5 48.4 all-reduce.17
  164.2 42.9 all-reduce.19
  214.8 176.7 all-reduce.23
  409.1 48.2 all-reduce.21
  462.8 202.5 all-reduce.25
where the time goes:
time: 805 us; the launch traced here: 794 us
  waiting for transfers between devices  310 us (39%)
  starting transfers between devices  213 us (26%)
  blocking collectives  134 us (17%)
  matrix products  52 us (6%)
  local copies, waits for them, and re-layouts  50.8 us (6%)
  other arithmetic  17.8 us (2%)
  between operations  16.8 us (2%)
    psum x1, waiting for transfers between devices, tied_whole(): return lax.psum(running_partial_sum, 'rows')  177 us
    unnamed x49, starting transfers between devices  147 us
    unnamed x1, blocking collectives  134 us
    psum x3, waiting for transfers between devices, residual_norm_backward(): lax.psum(running_partial_sum.astype(jnp.bfloat16), 'heads')  79 us
    unnamed x104, local copies, waits for them, and re-layouts  27.3 us
  transfers between devices with their start and end apart: 61, of which 16 were waited for; matrix products, arithmetic and copies ran while one was open for 25% of the time, Pallas kernels for 0%

commit v1 on v0

v1 whole, which is shorter than its diff:
```python
import math

import jax
import jax.numpy as jnp
from jax import lax
from jax.sharding import PartitionSpec as P

DH = 64
eps = 1e-05
f32 = jnp.float32
bf16 = jnp.bfloat16


def layer_norm_forward(values, gain):
    full = values.astype(f32)
    centered = full - jnp.mean(full, axis=-1, keepdims=True)
    inverse = lax.rsqrt(jnp.mean(centered * centered, axis=-1, keepdims=True) + eps)
    xhat = centered * inverse
    return (xhat * gain).astype(bf16), xhat, inverse


def layer_norm_backward(dn, xhat, inverse, gain):
    a = dn * gain
    first = jnp.mean(a, axis=-1, keepdims=True)
    second = jnp.mean(a * xhat, axis=-1, keepdims=True)
    return inverse * (a - first - xhat * second)


def gelu_slope(hpre):
    return 0.5 * (1.0 + jax.scipy.special.erf(hpre / math.sqrt(2.0))) + hpre * jnp.exp(
        -0.5 * hpre * hpre
    ) / math.sqrt(2.0 * math.pi)


def softmax_rows(scores):
    top = jnp.max(scores, axis=-1, keepdims=True)
    expo = jnp.exp(scores - top)
    return expo / jnp.sum(expo, axis=-1, keepdims=True)


def softmax_back(probs, dprobs, scale):
    inner = jnp.sum(probs * dprobs, axis=-1, keepdims=True)
    return (probs * (dprobs - inner) * scale).astype(bf16)


def dot(left, right):
    return jnp.dot(left, right, preferred_element_type=f32)


def contract_rows(left, right):
    return lax.dot_general(left, right, (((0,), (0,)), ((), ())), preferred_element_type=f32)


def contract_cols(left, right):
    return lax.dot_general(left, right, (((1,), (1,)), ((), ())), preferred_element_type=f32)


def einsum(spec, *args):
    return jnp.einsum(spec, *args, preferred_element_type=f32)


class Plan:
    def __init__(self, mesh):
        self.heads = mesh.shape["heads"]
        self.rows = mesh.shape["rows"]
        self.ys = 4
        self.zs = self.rows // (2 * self.ys)
        self.z_groups = [
            [z * 2 * self.ys + rest for z in range(self.zs)] for rest in range(2 * self.ys)
        ]

    def shift_heads(self, x, k):
        n = self.heads
        return lax.ppermute(x, "heads", [(i, (i + k) % n) for i in range(n)])

    def rotate(self, x):
        twice = jnp.concatenate([x, x], axis=0)
        return lax.dynamic_slice_in_dim(twice, lax.axis_index("heads"), x.shape[0], axis=0)

    def scatter_heads(self, part):
        narrow = part.astype(bf16)
        own = part[0]
        for k in range(1, self.heads):
            own = own + self.shift_heads(narrow[k], k).astype(f32)
        return own

    def gather_heads(self, own):
        return jnp.stack([own] + [self.shift_heads(own, -k) for k in range(1, self.heads)])

    def all_to_all(self, x, groups=None):
        return lax.all_to_all(
            x, "rows", split_axis=0, concat_axis=0, tiled=True, axis_index_groups=groups
        )

    def scatter_weights(self, parts):
        index = lax.axis_index("rows")
        core = index % 2
        y = (index // 2) % self.ys
        zs, ys = self.zs, self.ys
        flat = []
        for g in parts:
            share = g.shape[0] // self.rows
            flat.append(g.astype(bf16).reshape(zs, ys, 2, share * g.shape[1] // 128, 128))
        g = jnp.concatenate(flat, axis=3) if len(flat) > 1 else flat[0]
        kept = lax.dynamic_index_in_dim(g, core, 2, keepdims=False)
        sent = lax.dynamic_index_in_dim(g, 1 - core, 2, keepdims=False)
        pair = [(i, i ^ 1) for i in range(self.rows)]
        g = kept.astype(f32) + lax.ppermute(sent, "rows", pair).astype(f32)
        narrow = g.astype(bf16)
        total = lax.dynamic_index_in_dim(g, y, 1, keepdims=False)
        for k in range(1, ys):
            out = lax.dynamic_index_in_dim(narrow, (y + k) % ys, 1, keepdims=False)
            ring = [
                (i, (i // (2 * ys)) * 2 * ys + ((i // 2 + k) % ys) * 2 + i % 2)
                for i in range(self.rows)
            ]
            total = total + lax.ppermute(out, "rows", ring).astype(f32)
        got = self.all_to_all(total.astype(bf16), self.z_groups)
        done = jnp.sum(got.astype(f32), axis=0)
        outs = []
        at = 0
        for g in parts:
            share = g.shape[0] // self.rows
            size = share * g.shape[1] // 128
            outs.append(done[at : at + size].reshape(share, g.shape[1]))
            at += size
        return outs


def column_scores(queries, keys):
    scale = 1.0 / math.sqrt(DH)
    return softmax_rows(einsum("rhd,shd->hrs", queries, keys) * scale)


def solution(mesh):
    plan = Plan(mesh)

    def per_device(
        row_layer_input,
        column_layer_input,
        feedforward_layer_input,
        grad_out,
        layer_norm_gains,
        row_qkv,
        row_out,
        col_qkv,
        col_out,
        ffn_up,
        ffn_down,
    ):
        seqs, cols, width = row_layer_input.shape
        tokens = seqs * cols
        local = col_out.shape[1]
        heads = local // DH
        x2 = plan.rotate(feedforward_layer_input)
        go = plan.rotate(grad_out)
        x1 = plan.rotate(column_layer_input)
        x0 = plan.rotate(row_layer_input)
        go_flat = go.reshape(tokens, width)

        n2, xhat2, inv2 = layer_norm_forward(x2, layer_norm_gains[2])
        n2 = n2.reshape(tokens, width)
        hpre = dot(n2, ffn_up)
        act = jax.nn.gelu(hpre, approximate=False).astype(bf16)
        dpre = (dot(go_flat, ffn_down) * gelu_slope(hpre)).astype(bf16)
        dn2 = contract_cols(dpre, ffn_up).reshape(seqs, cols, width)
        sum2 = plan.scatter_heads(dn2)
        gz_own = go[0].astype(f32) + layer_norm_backward(
            sum2, xhat2[0], inv2[0], layer_norm_gains[2]
        )
        gz = plan.gather_heads(gz_own.astype(bf16)).reshape(tokens, width)

        n1, xhat1, inv1 = layer_norm_forward(x1, layer_norm_gains[1])
        n1 = n1.reshape(tokens, width)
        col_flat = col_qkv.reshape(width, 3 * local)
        col_all = dot(n1, col_flat).astype(bf16)

        def to_columns(x):
            wide = x.shape[1]
            x = jnp.swapaxes(x.reshape(seqs, cols, wide), 0, 1)
            x = plan.all_to_all(x.reshape(cols, seqs * wide // 128, 128))
            return x.reshape(cols * seqs, wide)

        def to_rows(x):
            wide = x.shape[1]
            x = plan.all_to_all(x.reshape(cols, seqs * wide // 128, 128))
            return jnp.swapaxes(x.reshape(cols, seqs, wide), 0, 1).reshape(tokens, wide)

        in_col = to_columns(col_all).reshape(tokens, 3, heads, DH)
        cq, ck, cv = in_col[:, 0], in_col[:, 1], in_col[:, 2]
        cprobs = column_scores(cq, ck)
        cprobs_bf = cprobs.astype(bf16)
        catt = einsum("hrs,shd->rhd", cprobs_bf, cv).astype(bf16)
        cog = dot(gz, col_out).astype(bf16)
        cog = to_columns(cog).reshape(tokens, heads, DH)
        cdprobs = einsum("rhd,shd->hrs", cog, cv)
        cds = softmax_back(cprobs, cdprobs, 1.0 / math.sqrt(DH))
        cdq = einsum("hrs,shd->rhd", cds, ck).astype(bf16)
        cdk = einsum("hrs,rhd->shd", cds, cq).astype(bf16)
        cdv = einsum("hrs,rhd->shd", cprobs_bf, cog).astype(bf16)
        back = jnp.concatenate(
            [item.reshape(tokens, local) for item in (cdq, cdk, cdv, catt)], axis=1
        )
        back = to_rows(back)
        col_d = back[:, : 3 * local]
        col_att = back[:, 3 * local :]
        dn1 = contract_cols(col_d, col_flat).reshape(seqs, cols, width)
        sum1 = plan.scatter_heads(dn1)
        gy_own = gz_own + layer_norm_backward(sum1, xhat1[0], inv1[0], layer_norm_gains[1])
        gy = plan.gather_heads(gy_own.astype(bf16)).reshape(tokens, width)

        n0, xhat0, inv0 = layer_norm_forward(x0, layer_norm_gains[0])
        n0 = n0.reshape(tokens, width)
        row_flat = row_qkv.reshape(width, 3 * local)
        row_all = dot(n0, row_flat).astype(bf16).reshape(seqs, cols, 3, heads, DH)
        rq, rk, rv = row_all[:, :, 0], row_all[:, :, 1], row_all[:, :, 2]
        row_scale = 1.0 / math.sqrt(DH * seqs * plan.rows)
        logits = lax.psum(einsum("sihd,sjhd->hij", rq, rk) * row_scale, "rows")
        rprobs = softmax_rows(logits)
        rprobs_bf = rprobs.astype(bf16)
        ratt = einsum("hij,sjhd->sihd", rprobs_bf, rv).astype(bf16).reshape(tokens, local)
        rog = dot(gy, row_out).astype(bf16).reshape(seqs, cols, heads, DH)
        dprobs = einsum("sihd,sjhd->hij", rog, rv)
        rdv = einsum("hij,sihd->sjhd", rprobs_bf, rog).astype(bf16).reshape(tokens, local)
        share = heads * cols // plan.rows
        mine = jnp.sum(plan.all_to_all(dprobs.reshape(plan.rows, share * cols)), axis=0)
        start = lax.axis_index("rows") * share
        probs_mine = lax.dynamic_slice_in_dim(rprobs.reshape(heads * cols, cols), start, share, 0)
        dl_mine = softmax_back(probs_mine, mine.reshape(share, cols), row_scale)
        spread = jnp.broadcast_to(dl_mine.reshape(1, share * cols), (plan.rows, share * cols))
        dlogits = plan.all_to_all(spread).reshape(heads, cols, cols)
        rdq = einsum("hij,sjhd->sihd", dlogits, rk).astype(bf16).reshape(tokens, local)
        rdk = einsum("hij,sihd->sjhd", dlogits, rq).astype(bf16).reshape(tokens, local)
        row_d = jnp.concatenate([rdq, rdk, rdv], axis=1)
        dn0 = contract_cols(row_d, row_flat).reshape(seqs, cols, width)
        sum0 = plan.scatter_heads(dn0)
        gx_own = gy_own + layer_norm_backward(sum0, xhat0[0], inv0[0], layer_norm_gains[0])
        gx = plan.gather_heads(gx_own.astype(bf16))
        twice = jnp.concatenate([gx, gx], axis=0)
        turn = (seqs - lax.axis_index("heads")) % seqs
        input_gradient = lax.dynamic_slice_in_dim(twice, turn, seqs, axis=0)

        g_up, g_down = plan.scatter_weights([contract_rows(n2, dpre), contract_rows(go_flat, act)])
        g_cqkv, g_cout = plan.scatter_weights(
            [contract_rows(n1, col_d), contract_rows(gz, col_att)]
        )
        g_rqkv, g_rout = plan.scatter_weights([contract_rows(n0, row_d), contract_rows(gy, ratt)])
        return (
            input_gradient,
            g_rqkv.reshape(-1, 3, local),
            g_rout,
            g_cqkv.reshape(-1, 3, local),
            g_cout,
            g_up,
            g_down,
        )

    return jax.shard_map(
        per_device,
        mesh=mesh,
        in_specs=(
            P("rows", None, None),
            P("rows", None, None),
            P("rows", None, None),
            P("rows", None, None),
            P(),
            P(None, None, "heads"),
            P(None, "heads"),
            P(None, None, "heads"),
            P(None, "heads"),
            P(None, "heads"),
            P(None, "heads"),
        ),
        out_specs=(
            P("rows", None, None),
            P("rows", None, "heads"),
            P("rows", "heads"),
            P("rows", None, "heads"),
            P("rows", "heads"),
            P("rows", "heads"),
            P("rows", "heads"),
        ),
        check_vma=False,
    )
```

time: 805 us -> 544 us (0.68)
  waiting for transfers between devices: 310 us -> 57.2 us
  starting transfers between devices: 213 us -> 110 us
  blocking collectives: 134 us -> 233 us
  local copies, waits for them, and re-layouts: 50.8 us -> 71.6 us
  matrix products: 52 us -> 32.6 us
  between operations: 16.8 us -> 1.96 us
  other arithmetic: 17.8 us -> 27.7 us
    psum x4 -> x0, waiting for transfers between devices: 256 us -> none  [the longest x1 177 us: tied_whole(): return lax.psum(running_partial_sum, 'rows')]
    psum x0 -> x1, blocking collectives: none -> 233 us  [per_device(): logits = lax.psum(einsum('sihd,sjhd->hij', rq, rk) * row_scale, 'rows')]
    unnamed x49 -> x0, starting transfers between devices: 147 us -> none
    unnamed x1 -> x0, blocking collectives: 134 us -> none
    ppermute x0 -> x30, starting transfers between devices: none -> 36.3 us  [the longest x18 23.5 us: shift_heads(): return lax.ppermute(x, 'heads', [(i, (i + k) % n) for i in range(n)])]
    ppermute x0 -> x30, waiting for transfers between devices: none -> 20.6 us  [the longest x18 13.8 us: shift_heads(): return lax.ppermute(x, 'heads', [(i, (i + k) % n) for i in range(n)])]
    reshape x22 -> x27, local copies, waits for them, and re-layouts: 10.1 us -> 28.2 us  [the longest x6 8.04 us: scatter_weights(): g.astype(bf16).reshape(zs, ys, 2, share * g.shape[1] // 128, 128)]
    unnamed x104 -> x77, local copies, waits for them, and re-layouts: 27.3 us -> 13.8 us
  transfers between devices with their start and end apart: 61 -> 38, of which waited for: 16 -> 17; matrix products, arithmetic and copies ran while one was open for 25% -> 22% of each run, Pallas kernels for 0% -> 0%
where the time goes in v1:
time: 544 us; the launch traced here: 534 us
  blocking collectives  233 us (43%)
  starting transfers between devices  110 us (20%)
  local copies, waits for them, and re-layouts  71.6 us (13%)
  waiting for transfers between devices  57.2 us (11%)
  matrix products  32.6 us (6%)
  other arithmetic  27.7 us (5%)
    psum x1, blocking collectives, per_device(): logits = lax.psum(einsum('sihd,sjhd->hij', rq, rk) * row_scale, 'rows')  233 us
    all_to_all x8, starting transfers between devices, all_to_all(): lax.all_to_all(x, 'rows', split_axis=0, concat_axis=0, tiled=True, axis_i...  73.2 us
    all_to_all x8, waiting for transfers between devices, all_to_all(): lax.all_to_all(x, 'rows', split_axis=0, concat_axis=0, tiled=True, axis_i...  36.6 us
    ppermute x18, starting transfers between devices, shift_heads(): return lax.ppermute(x, 'heads', [(i, (i + k) % n) for i in range(n)])  23.5 us
    dot_general x11, matrix products, einsum(): return jnp.einsum(spec, *args, preferred_element_type=f32)  17 us
    ppermute x18, waiting for transfers between devices, shift_heads(): return lax.ppermute(x, 'heads', [(i, (i + k) % n) for i in range(n)])  13.8 us
    unnamed x77, local copies, waits for them, and re-layouts  13.8 us
    ppermute x9, starting transfers between devices, scatter_weights(): total = total + lax.ppermute(out, 'rows', ring).astype(f32)  12.7 us
  transfers between devices with their start and end apart: 38, of which 17 were waited for; matrix products, arithmetic and copies ran while one was open for 22% of the time, Pallas kernels for 0%

profile of v1, /device:TPU:32, one launch (start us, length us, event | category | flops | bytes accessed | tf_op | source)
XLA Modules:
  0.0 534.0 jit_solution(2541354798619557868)
XLA Ops:
  8.4 2.8 collective-permute-start.2
  13.4 3.1 convolution_convert_fusion
  17.7 2.6 reshape.332
  30.4 1.9 fusion.204
  32.2 1.8 collective-permute-start.5
  34.0 2.4 collective-permute-start.4
  39.0 2.0 copy.100
  41.0 2.2 reshape.302
  44.2 1.7 copy.150
  46.0 1.7 copy.149
  51.6 1.7 copy.104
  53.3 1.7 reshape.305
  55.0 12.0 %all-to-all-start.1 = ((bf16[64,6,128]{2,1,0:T(8,128)(2,1)}), bf16[64,6,128]{2,1,0:T(8,128)(2,1)}, u32[]{:S(2)}, u32[]{:S(2)}) async-start(bf16[64,6,128]{2,1,0:T(8,128)(2,1)} %reshape.305), calls=%async_computation.1 | async-start | bytes 262144 | tf_op jit(solution)/shard_map/all_to_all | solution.py:91
  67.0 1.8 fusion.16
  68.8 233.3 %psum.7 = f32[3,64,64]{2,1,0:T(8,128)S(1)} all-reduce(f32[3,64,64]{2,1,0:T(8,128)} %fusion.16), channel_id=1, replica_groups=mesh['rows'=64,'heads'=4] {'rows'}, use_global_device_ids=true, to_apply=%region_13.0 | all-reduce | flops 12288 | bytes 98304 | tf_op jit(solution)/shard_map/psum | solution.py:218
  302.1 23.8 %all-to-all-start = ((bf16[64,18,128]{2,1,0:T(8,128)(2,1)}), bf16[64,18,128]{2,1,0:T(8,128)(2,1)}, u32[]{:S(2)}, u32[]{:S(2)}) async-start(bf16[64,18,128]{2,1,0:T(8,128)(2,1)} %reshape.302), calls=%async_computation | async-start | bytes 786432 | tf_op jit(solution)/shard_map/all_to_all | solution.py:91
  326.6 1.9 fusion.13
  328.5 1.8 reshape_reshape.13
  330.3 1.7 copy.106
  332.0 8.0 %all-to-all-done = bf16[64,18,128]{2,1,0:T(8,128)(2,1)} async-done(((bf16[64,18,128]{2,1,0:T(8,128)(2,1)}), bf16[64,18,128]{2,1,0:T(8,128)(2,1)}, u32[]{:S(2)}, u32[]{:S(2)}) %all-to-all-start) | async-done | bytes 294944 | tf_op jit(solution)/shard_map/all_to_all | solution.py:91
  340.0 2.4 reshape_reshape.12
  342.4 2.2 fusion.208
  344.6 1.7 copy.147
  346.3 1.7 copy.146
  348.1 1.7 copy.145
  349.8 2.3 fusion.215
  352.0 2.2 convolution_convert_fusion.13
  354.3 1.6 copy.115
  355.9 2.2 convolution_convert_fusion.14
  358.2 1.6 copy.114
  359.8 2.2 fusion.122
  362.0 2.9 convolution_convert_fusion.15
  364.9 1.7 copy.113
  366.5 2.9 convolution_convert_fusion.16
  369.4 1.6 copy.112
  371.0 2.0 pad_maximum_fusion.1
  373.0 2.1 reshape.310
  375.1 7.1 %all-to-all-start.2 = ((bf16[64,24,128]{2,1,0:T(8,128)(2,1)}), bf16[64,24,128]{2,1,0:T(8,128)(2,1)}, u32[]{:S(2)}, u32[]{:S(2)}) async-start(bf16[64,24,128]{2,1,0:T(8,128)(2,1)} %reshape.310), calls=%async_computation.2 | async-start | bytes 786432 | tf_op jit(solution)/shard_map/all_to_all | solution.py:91
  382.9 1.8 copy.130
  384.7 1.8 reshape.325
  386.9 3.1 fusion.197
  391.0 2.7 collective-permute-start.29
  394.5 1.5 all-to-all-done.2
  402.1 2.0 collective-permute-start.7
  408.4 1.5 collective-permute-start.27
  413.6 3.0 collective-permute-start.10
  418.6 2.1 fusion.54
  423.4 7.7 %all-to-all-start.3 = ((f32[64,1,192]{2,1,0:T(1,128)}), f32[64,1,192]{2,1,0:T(1,128)S(1)}, u32[]{:S(2)}, u32[]{:S(2)}) async-start(f32[64,1,192]{2,1,0:T(1,128)} %all_to_all.37), calls=%async_computation.3 | async-start | bytes 131072 | tf_op jit(solution)/shard_map/all_to_all | solution.py:91
  431.4 8.9 %all-to-all-done.3 = f32[64,1,192]{2,1,0:T(1,128)S(1)} async-done(((f32[64,1,192]{2,1,0:T(1,128)}), f32[64,1,192]{2,1,0:T(1,128)S(1)}, u32[]{:S(2)}, u32[]{:S(2)}) %all-to-all-start.3) | async-done | bytes 49184 | tf_op jit(solution)/shard_map/all_to_all | solution.py:91
  441.4 5.4 %all-to-all-start.4 = ((bf16[64,1,192]{2,1,0:T(2,128)(2,1)}), bf16[64,1,192]{2,1,0:T(2,128)(2,1)S(1)}, u32[]{:S(2)}, u32[]{:S(2)}) async-start(bf16[64,1,192]{2,1,0:T(2,128)(2,1)} %broadcast_in_dim.5), calls=%async_computation.4 | async-start | bytes 131072 | tf_op jit(solution)/shard_map/all_to_all | solution.py:91
  448.9 7.2 %all-to-all-done.4 = bf16[64,1,192]{2,1,0:T(2,128)(2,1)S(1)} async-done(((bf16[64,1,192]{2,1,0:T(2,128)(2,1)}), bf16[64,1,192]{2,1,0:T(2,128)(2,1)S(1)}, u32[]{:S(2)}, u32[]{:S(2)}) %all-to-all-start.4) | async-done | bytes 24608 | tf_op jit(solution)/shard_map/all_to_all | solution.py:91
  456.1 5.2 all-to-all-start.7
  465.1 2.1 collective-permute-start.14
  471.7 2.7 collective-permute-done.13
  480.9 2.2 collective-permute-done.15
  483.2 2.7 collective-permute-done.16
  485.9 1.8 collective-permute-done.17
  490.8 1.7 collective-permute-start.24
  493.0 3.2 collective-permute-start.21
  499.1 4.7 collective-permute-done.23
  504.5 7.2 %all-to-all-start.6 = ((bf16[8,72,128]{2,1,0:T(8,128)(2,1)}), bf16[8,72,128]{2,1,0:T(8,128)(2,1)S(1)}, u32[]{:S(2)}, u32[]{:S(2)}) async-start(bf16[8,72,128]{2,1,0:T(8,128)(2,1)} %fusion.94), calls=%async_computation.6 | async-start | bytes 294912 | tf_op jit(solution)/shard_map/all_to_all | solution.py:91
  513.6 5.9 %all-to-all-done.6 = bf16[8,72,128]{2,1,0:T(8,128)(2,1)S(1)} async-done(((bf16[8,72,128]{2,1,0:T(8,128)(2,1)}), bf16[8,72,128]{2,1,0:T(8,128)(2,1)S(1)}, u32[]{:S(2)}, u32[]{:S(2)}) %all-to-all-start.6) | async-done | bytes 147488 | tf_op jit(solution)/shard_map/all_to_all | solution.py:91
  519.5 4.7 all-to-all-start.5
  527.0 5.1 all-to-all-done.5
  (232 shorter events, 82.1 us)
Async XLA Ops:
  0.6 3.8 copy-start
  0.6 2.4 copy-start.21
  3.1 1.3 copy-start.28
  3.3 10.1 %copy-start.19 = (bf16[4,64,768]{2,1,0:T(8,128)(2,1)}, bf16[4,64,768]{2,1,0:T(8,128)(2,1)S(1)}, u32[]{:S(2)}) copy-start(bf16[4,64,768]{2,1,0:T(8,128)(2,1)S(1)} %fusion.59) | copy-start | bytes 1179652
  4.4 1.3 copy-start.30
  8.4 20.5 %collective-permute-start.2 = (bf16[64,768]{1,0:T(8,128)(2,1)}, bf16[64,768]{1,0:T(8,128)(2,1)}, u32[]{:S(2)}, u32[]{:S(2)}) collective-permute-start(bf16[64,768]{1,0:T(8,128)(2,1)} %get-tuple-element.65), channel_id=1, source_target_pairs={{0,3},{1,0},{2,1},{3,2},{4,7},{5,4},{6,5},{7,6},{8,11},{9,8},{10,9... | collective-permute-start | bytes 294920 | tf_op jit(solution)/shard_map/ppermute | solution.py:74
  11.2 17.8 %collective-permute-start.1 = (bf16[64,768]{1,0:T(8,128)(2,1)}, bf16[64,768]{1,0:T(8,128)(2,1)}, u32[]{:S(2)}, u32[]{:S(2)}) collective-permute-start(bf16[64,768]{1,0:T(8,128)(2,1)} %get-tuple-element.66), channel_id=1, source_target_pairs={{0,2},{1,3},{2,0},{3,1},{4,6},{5,7},{6,4},{7,5},{8,10},{9,11},{10,... | collective-permute-start | bytes 294920 | tf_op jit(solution)/shard_map/ppermute | solution.py:74
  11.9 17.0 %collective-permute-start = (bf16[64,768]{1,0:T(8,128)(2,1)}, bf16[64,768]{1,0:T(8,128)(2,1)}, u32[]{:S(2)}, u32[]{:S(2)}) collective-permute-start(bf16[64,768]{1,0:T(8,128)(2,1)} %get-tuple-element.64), channel_id=1, source_target_pairs={{0,1},{1,2},{2,3},{3,0},{4,5},{5,6},{6,7},{7,4},{8,9},{9,10},{10,1... | collective-permute-start | bytes 294920 | tf_op jit(solution)/shard_map/ppermute | solution.py:74
  21.6 365.3 %collective-permute-start.26 = (bf16[8,4,144,128]{3,2,1,0:T(8,128)(2,1)}, bf16[8,4,144,128]{3,2,1,0:T(8,128)(2,1)}, u32[]{:S(2)}, u32[]{:S(2)}) collective-permute-start(bf16[8,4,144,128]{3,2,1,0:T(8,128)(2,1)} %dynamic-slice_bitcast_fusion), channel_id=1, source_target_pairs={{0,4},{4,0},{8,12},{12,8},{16,20},{20,16},{24,28},{28,24},{32,36},... | collective-permute-start | bytes 3538952 | tf_op jit(solution)/shard_map/ppermute | solution.py:108
  23.1 1.5 copy-start.27
  23.2 1.5 copy-start.2
  24.6 2.0 copy-start.5
  24.6 2.0 copy-start.7
  24.6 1.6 copy-start.3
  28.9 8.2 %copy-start.12 = (bf16[4,64,3,3,64]{1,0,4,3,2:T(4,128)(2,1)S(1)}, bf16[4,64,3,3,64]{1,0,4,3,2:T(4,128)(2,1)}, u32[]{:S(2)}) copy-start(bf16[4,64,3,3,64]{1,0,4,3,2:T(4,128)(2,1)} %reshape.315) | copy-start | bytes 884740
  30.3 7.8 %copy-start.16 = (bf16[256,576]{0,1:T(8,128)(2,1)S(1)}, bf16[256,576]{0,1:T(8,128)(2,1)}, u32[]{:S(2)}) copy-start(bf16[256,576]{0,1:T(8,128)(2,1)} %convolution_convert_fusion.7) | copy-start | bytes 884740
  32.2 15.5 %collective-permute-start.5 = (bf16[64,768]{1,0:T(8,128)(2,1)}, bf16[64,768]{1,0:T(8,128)(2,1)}, u32[]{:S(2)}, u32[]{:S(2)}) collective-permute-start(bf16[64,768]{1,0:T(8,128)(2,1)} %get-tuple-element.30), channel_id=1, source_target_pairs={{0,1},{1,2},{2,3},{3,0},{4,5},{5,6},{6,7},{7,4},{8,9},{9,10},{10,1... | collective-permute-start | bytes 294920 | tf_op jit(solution)/shard_map/ppermute | solution.py:74
  34.0 13.7 %collective-permute-start.4 = (bf16[64,768]{1,0:T(8,128)(2,1)}, bf16[64,768]{1,0:T(8,128)(2,1)}, u32[]{:S(2)}, u32[]{:S(2)}) collective-permute-start(bf16[64,768]{1,0:T(8,128)(2,1)} %get-tuple-element.30), channel_id=1, source_target_pairs={{0,2},{1,3},{2,0},{3,1},{4,6},{5,7},{6,4},{7,5},{8,10},{9,11},{10,... | collective-permute-start | bytes 294920 | tf_op jit(solution)/shard_map/ppermute | solution.py:74
  36.5 11.3 %collective-permute-start.3 = (bf16[64,768]{1,0:T(8,128)(2,1)}, bf16[64,768]{1,0:T(8,128)(2,1)}, u32[]{:S(2)}, u32[]{:S(2)}) collective-permute-start(bf16[64,768]{1,0:T(8,128)(2,1)} %get-tuple-element.30), channel_id=1, source_target_pairs={{0,3},{1,0},{2,1},{3,2},{4,7},{5,4},{6,5},{7,6},{8,11},{9,8},{10,9... | collective-permute-start | bytes 294920 | tf_op jit(solution)/shard_map/ppermute | solution.py:74
  55.0 247.1 %all-to-all-start.1 = ((bf16[64,6,128]{2,1,0:T(8,128)(2,1)}), bf16[64,6,128]{2,1,0:T(8,128)(2,1)}, u32[]{:S(2)}, u32[]{:S(2)}) async-start(bf16[64,6,128]{2,1,0:T(8,128)(2,1)} %reshape.305), calls=%async_computation.1 | async-start | bytes 262144 | tf_op jit(solution)/shard_map/all_to_all | solution.py:91
  302.1 37.9 %all-to-all-start = ((bf16[64,18,128]{2,1,0:T(8,128)(2,1)}), bf16[64,18,128]{2,1,0:T(8,128)(2,1)}, u32[]{:S(2)}, u32[]{:S(2)}) async-start(bf16[64,18,128]{2,1,0:T(8,128)(2,1)} %reshape.302), calls=%async_computation | async-start | bytes 786432 | tf_op jit(solution)/shard_map/all_to_all | solution.py:91
  375.1 20.9 %all-to-all-start.2 = ((bf16[64,24,128]{2,1,0:T(8,128)(2,1)}), bf16[64,24,128]{2,1,0:T(8,128)(2,1)}, u32[]{:S(2)}, u32[]{:S(2)}) async-start(bf16[64,24,128]{2,1,0:T(8,128)(2,1)} %reshape.310), calls=%async_computation.2 | async-start | bytes 786432 | tf_op jit(solution)/shard_map/all_to_all | solution.py:91
  391.0 22.6 %collective-permute-start.29 = (bf16[8,144,128]{2,1,0:T(8,128)(2,1)}, bf16[8,144,128]{2,1,0:T(8,128)(2,1)}, u32[]{:S(2)}, u32[]{:S(2)}) collective-permute-start(bf16[8,144,128]{2,1,0:T(8,128)(2,1)} %get-tuple-element.38), channel_id=1, source_target_pairs={{0,24},{4,28},{8,0},{12,4},{16,8},{20,12},{24,16},{28,20},{32,56},... | collective-permute-start | bytes 884744 | tf_op jit(solution)/shard_map/ppermute | solution.py:117
  393.7 22.9 %collective-permute-start.28 = (bf16[8,144,128]{2,1,0:T(8,128)(2,1)}, bf16[8,144,128]{2,1,0:T(8,128)(2,1)}, u32[]{:S(2)}, u32[]{:S(2)}) collective-permute-start(bf16[8,144,128]{2,1,0:T(8,128)(2,1)} %get-tuple-element.39), channel_id=1, source_target_pairs={{0,16},{4,20},{8,24},{12,28},{16,0},{20,4},{24,8},{28,12},{32,48},... | collective-permute-start | bytes 884744 | tf_op jit(solution)/shard_map/ppermute | solution.py:117
  397.2 1.4 copy-start.8
  400.7 7.1 %collective-permute-start.8 = (bf16[64,768]{1,0:T(8,128)(2,1)S(1)}, bf16[64,768]{1,0:T(8,128)(2,1)S(1)}, u32[]{:S(2)}, u32[]{:S(2)}) collective-permute-start(bf16[64,768]{1,0:T(8,128)(2,1)S(1)} %get-tuple-element.62), channel_id=1, source_target_pairs={{0,3},{1,0},{2,1},{3,2},{4,7},{5,4},{6,5},{7,6},{8,11},{9,8},{10,9... | collective-permute-start | bytes 294920 | tf_op jit(solution)/shard_map/ppermute | solution.py:74
  402.1 7.8 %collective-permute-start.7 = (bf16[64,768]{1,0:T(8,128)(2,1)}, bf16[64,768]{1,0:T(8,128)(2,1)}, u32[]{:S(2)}, u32[]{:S(2)}) collective-permute-start(bf16[64,768]{1,0:T(8,128)(2,1)} %get-tuple-element.63), channel_id=1, source_target_pairs={{0,2},{1,3},{2,0},{3,1},{4,6},{5,7},{6,4},{7,5},{8,10},{9,11},{10,... | collective-permute-start | bytes 294920 | tf_op jit(solution)/shard_map/ppermute | solution.py:74
  404.1 7.0 %collective-permute-start.6 = (bf16[64,768]{1,0:T(8,128)(2,1)}, bf16[64,768]{1,0:T(8,128)(2,1)}, u32[]{:S(2)}, u32[]{:S(2)}) collective-permute-start(bf16[64,768]{1,0:T(8,128)(2,1)} %get-tuple-element.61), channel_id=1, source_target_pairs={{0,1},{1,2},{2,3},{3,0},{4,5},{5,6},{6,7},{7,4},{8,9},{9,10},{10,1... | collective-permute-start | bytes 294920 | tf_op jit(solution)/shard_map/ppermute | solution.py:74
  406.2 2.2 copy-start.25
  406.2 4.9 copy-start.15
  406.7 5.6 %copy-start.17 = (f32[64,768]{1,0:T(8,128)S(1)}, f32[64,768]{1,0:T(8,128)}, u32[]{:S(2)}) copy-start(f32[64,768]{1,0:T(8,128)} %get-tuple-element.31) | copy-start | bytes 589828
  408.4 10.2 %collective-permute-start.27 = (bf16[8,144,128]{2,1,0:T(8,128)(2,1)S(1)}, bf16[8,144,128]{2,1,0:T(8,128)(2,1)S(1)}, u32[]{:S(2)}, u32[]{:S(2)}) collective-permute-start(bf16[8,144,128]{2,1,0:T(8,128)(2,1)S(1)} %copy-done.25), channel_id=1, source_target_pairs={{0,8},{4,12},{8,16},{12,20},{16,24},{20,28},{24,0},{28,4},{32,40},... | collective-permute-start | bytes 884744 | tf_op jit(solution)/shard_map/ppermute | solution.py:117
  409.9 78.7 %collective-permute-start.22 = (bf16[8,4,72,128]{3,2,1,0:T(8,128)(2,1)}, bf16[8,4,72,128]{3,2,1,0:T(8,128)(2,1)}, u32[]{:S(2)}, u32[]{:S(2)}) collective-permute-start(bf16[8,4,72,128]{3,2,1,0:T(8,128)(2,1)} %fusion.45), channel_id=1, source_target_pairs={{0,4},{4,0},{8,12},{12,8},{16,20},{20,16},{24,28},{28,24},{32,36},... | collective-permute-start | bytes 1769480 | tf_op jit(solution)/shard_map/ppermute | solution.py:108
  413.1 7.6 %collective-permute-start.11 = (bf16[64,768]{1,0:T(8,128)(2,1)S(1)}, bf16[64,768]{1,0:T(8,128)(2,1)S(1)}, u32[]{:S(2)}, u32[]{:S(2)}) collective-permute-start(bf16[64,768]{1,0:T(8,128)(2,1)S(1)} %get-tuple-element.25), channel_id=1, source_target_pairs={{0,1},{1,2},{2,3},{3,0},{4,5},{5,6},{6,7},{7,4},{8,9},{9,10},{10,1... | collective-permute-start | bytes 294920 | tf_op jit(solution)/shard_map/ppermute | solution.py:74
  413.6 8.3 %collective-permute-start.10 = (bf16[64,768]{1,0:T(8,128)(2,1)S(1)}, bf16[64,768]{1,0:T(8,128)(2,1)S(1)}, u32[]{:S(2)}, u32[]{:S(2)}) collective-permute-start(bf16[64,768]{1,0:T(8,128)(2,1)S(1)} %get-tuple-element.25), channel_id=1, source_target_pairs={{0,2},{1,3},{2,0},{3,1},{4,6},{5,7},{6,4},{7,5},{8,10},{9,11},{10,... | collective-permute-start | bytes 294920 | tf_op jit(solution)/shard_map/ppermute | solution.py:74
  416.6 5.3 collective-permute-start.9
  418.6 3.4 copy-start.24
  420.7 1.7 copy-start.14
  421.9 9.3 %copy-start.20 = (bf16[256,192]{0,1:T(8,128)(2,1)S(1)}, bf16[256,192]{0,1:T(8,128)(2,1)}, u32[]{:S(2)}) copy-start(bf16[256,192]{0,1:T(8,128)(2,1)} %reshape.325) | copy-start | bytes 294916
  423.4 16.9 %all-to-all-start.3 = ((f32[64,1,192]{2,1,0:T(1,128)}), f32[64,1,192]{2,1,0:T(1,128)S(1)}, u32[]{:S(2)}, u32[]{:S(2)}) async-start(f32[64,1,192]{2,1,0:T(1,128)} %all_to_all.37), calls=%async_computation.3 | async-start | bytes 131072 | tf_op jit(solution)/shard_map/all_to_all | solution.py:91
  441.4 14.6 %all-to-all-start.4 = ((bf16[64,1,192]{2,1,0:T(2,128)(2,1)}), bf16[64,1,192]{2,1,0:T(2,128)(2,1)S(1)}, u32[]{:S(2)}, u32[]{:S(2)}) async-start(bf16[64,1,192]{2,1,0:T(2,128)(2,1)} %broadcast_in_dim.5), calls=%async_computation.4 | async-start | bytes 131072 | tf_op jit(solution)/shard_map/all_to_all | solution.py:91
  447.4 14.4 %copy-start.13 = (bf16[4,64,1,3,64]{4,1,0,3,2:T(8,128)(2,1)S(1)}, bf16[4,64,1,3,64]{4,1,0,3,2:T(8,128)(2,1)}, u32[]{:S(2)}) copy-start(bf16[4,64,1,3,64]{4,1,0,3,2:T(8,128)(2,1)} %copy.149) | copy-start | bytes 294916
  456.1 48.4 %all-to-all-start.7 = ((bf16[8,144,128]{2,1,0:T(8,128)(2,1)}), bf16[8,144,128]{2,1,0:T(8,128)(2,1)}, u32[]{:S(2)}, u32[]{:S(2)}) async-start(bf16[8,144,128]{2,1,0:T(8,128)(2,1)} %fusion.54), calls=%async_computation.7 | async-start | bytes 589824 | tf_op jit(solution)/shard_map/all_to_all | solution.py:91
  461.8 1.2 copy-start.4
  463.0 5.3 copy-start.6
  465.1 6.6 %collective-permute-start.14 = (bf16[64,768]{1,0:T(8,128)(2,1)}, bf16[64,768]{1,0:T(8,128)(2,1)}, u32[]{:S(2)}, u32[]{:S(2)}) collective-permute-start(bf16[64,768]{1,0:T(8,128)(2,1)} %get-tuple-element.59), channel_id=1, source_target_pairs={{0,3},{1,0},{2,1},{3,2},{4,7},{5,4},{6,5},{7,6},{8,11},{9,8},{10,9... | collective-permute-start | bytes 294920 | tf_op jit(solution)/shard_map/ppermute | solution.py:74
  467.2 7.2 %collective-permute-start.13 = (bf16[64,768]{1,0:T(8,128)(2,1)}, bf16[64,768]{1,0:T(8,128)(2,1)}, u32[]{:S(2)}, u32[]{:S(2)}) collective-permute-start(bf16[64,768]{1,0:T(8,128)(2,1)} %get-tuple-element.60), channel_id=1, source_target_pairs={{0,2},{1,3},{2,0},{3,1},{4,6},{5,7},{6,4},{7,5},{8,10},{9,11},{10,... | collective-permute-start | bytes 294920 | tf_op jit(solution)/shard_map/ppermute | solution.py:74
  468.3 7.1 %collective-permute-start.12 = (bf16[64,768]{1,0:T(8,128)(2,1)S(1)}, bf16[64,768]{1,0:T(8,128)(2,1)}, u32[]{:S(2)}, u32[]{:S(2)}) collective-permute-start(bf16[64,768]{1,0:T(8,128)(2,1)S(1)} %get-tuple-element.58), channel_id=1, source_target_pairs={{0,1},{1,2},{2,3},{3,0},{4,5},{5,6},{6,7},{7,4},{8,9},{9,10},{10,1... | collective-permute-start | bytes 294920 | tf_op jit(solution)/shard_map/ppermute | solution.py:74
  469.3 7.4 %copy-start.18 = (f32[64,768]{1,0:T(8,128)S(1)}, f32[64,768]{1,0:T(8,128)}, u32[]{:S(2)}) copy-start(f32[64,768]{1,0:T(8,128)} %get-tuple-element.26) | copy-start | bytes 589828
  469.3 7.4 %copy-start.29 = (f32[64]{0:T(128)S(1)}, f32[64]{0:T(128)}, u32[]{:S(2)}) copy-start(f32[64]{0:T(128)} %slice_bitcast_fusion.4) | copy-start | bytes 772
  470.6 7.8 %copy-start.11 = (bf16[8,4,2,18,128]{4,3,2,1,0:T(8,128)(2,1)S(1)}, bf16[8,4,2,18,128]{4,3,2,1,0:T(8,128)(2,1)}, u32[]{:S(2)}) copy-start(bf16[8,4,2,18,128]{4,3,2,1,0:T(8,128)(2,1)} %reshape.326) | copy-start | bytes 884740
  477.8 5.4 %collective-permute-start.15 = (bf16[64,768]{1,0:T(8,128)(2,1)S(1)}, bf16[64,768]{1,0:T(8,128)(2,1)S(1)}, u32[]{:S(2)}, u32[]{:S(2)}) collective-permute-start(bf16[64,768]{1,0:T(8,128)(2,1)S(1)} %get-tuple-element.23), channel_id=1, source_target_pairs={{0,3},{1,0},{2,1},{3,2},{4,7},{5,4},{6,5},{7,6},{8,11},{9,8},{10,9... | collective-permute-start | bytes 294920 | tf_op jit(solution)/shard_map/ppermute | solution.py:74
  478.5 14.2 %collective-permute-start.18 = (bf16[8,4,72,128]{3,2,1,0:T(8,128)(2,1)S(1)}, bf16[8,4,72,128]{3,2,1,0:T(8,128)(2,1)S(1)}, u32[]{:S(2)}, u32[]{:S(2)}) collective-permute-start(bf16[8,4,72,128]{3,2,1,0:T(8,128)(2,1)S(1)} %fusion.49), channel_id=1, source_target_pairs={{0,4},{4,0},{8,12},{12,8},{16,20},{20,16},{24,28},{28,24},{32,36},... | collective-permute-start | bytes 1769480 | tf_op jit(solution)/shard_map/ppermute | solution.py:108
  478.6 7.2 %collective-permute-start.16 = (bf16[64,768]{1,0:T(8,128)(2,1)S(1)}, bf16[64,768]{1,0:T(8,128)(2,1)S(1)}, u32[]{:S(2)}, u32[]{:S(2)}) collective-permute-start(bf16[64,768]{1,0:T(8,128)(2,1)S(1)} %get-tuple-element.23), channel_id=1, source_target_pairs={{0,2},{1,3},{2,0},{3,1},{4,6},{5,7},{6,4},{7,5},{8,10},{9,11},{10,... | collective-permute-start | bytes 294920 | tf_op jit(solution)/shard_map/ppermute | solution.py:74
  480.1 7.6 %collective-permute-start.17 = (bf16[64,768]{1,0:T(8,128)(2,1)S(1)}, bf16[64,768]{1,0:T(8,128)(2,1)S(1)}, u32[]{:S(2)}, u32[]{:S(2)}) collective-permute-start(bf16[64,768]{1,0:T(8,128)(2,1)S(1)} %get-tuple-element.23), channel_id=1, source_target_pairs={{0,1},{1,2},{2,3},{3,0},{4,5},{5,6},{6,7},{7,4},{8,9},{9,10},{10,1... | collective-permute-start | bytes 294920 | tf_op jit(solution)/shard_map/ppermute | solution.py:74
  489.9 6.9 %collective-permute-start.25 = (bf16[8,72,128]{2,1,0:T(8,128)(2,1)S(1)}, bf16[8,72,128]{2,1,0:T(8,128)(2,1)S(1)}, u32[]{:S(2)}, u32[]{:S(2)}) collective-permute-start(bf16[8,72,128]{2,1,0:T(8,128)(2,1)S(1)} %get-tuple-element.44), channel_id=1, source_target_pairs={{0,24},{4,28},{8,0},{12,4},{16,8},{20,12},{24,16},{28,20},{32,56},... | collective-permute-start | bytes 442376 | tf_op jit(solution)/shard_map/ppermute | solution.py:117
  490.8 8.3 %collective-permute-start.24 = (bf16[8,72,128]{2,1,0:T(8,128)(2,1)S(1)}, bf16[8,72,128]{2,1,0:T(8,128)(2,1)S(1)}, u32[]{:S(2)}, u32[]{:S(2)}) collective-permute-start(bf16[8,72,128]{2,1,0:T(8,128)(2,1)S(1)} %get-tuple-element.45), channel_id=1, source_target_pairs={{0,16},{4,20},{8,24},{12,28},{16,0},{20,4},{24,8},{28,12},{32,48},... | collective-permute-start | bytes 442376 | tf_op jit(solution)/shard_map/ppermute | solution.py:117
  492.5 11.2 %collective-permute-start.23 = (bf16[8,72,128]{2,1,0:T(8,128)(2,1)S(1)}, bf16[8,72,128]{2,1,0:T(8,128)(2,1)S(1)}, u32[]{:S(2)}, u32[]{:S(2)}) collective-permute-start(bf16[8,72,128]{2,1,0:T(8,128)(2,1)S(1)} %get-tuple-element.43), channel_id=1, source_target_pairs={{0,8},{4,12},{8,16},{12,20},{16,24},{20,28},{24,0},{28,4},{32,40},... | collective-permute-start | bytes 442376 | tf_op jit(solution)/shard_map/ppermute | solution.py:117
  493.0 19.8 %collective-permute-start.21 = (bf16[8,72,128]{2,1,0:T(8,128)(2,1)S(1)}, bf16[8,72,128]{2,1,0:T(8,128)(2,1)S(1)}, u32[]{:S(2)}, u32[]{:S(2)}) collective-permute-start(bf16[8,72,128]{2,1,0:T(8,128)(2,1)S(1)} %get-tuple-element.47), channel_id=1, source_target_pairs={{0,24},{4,28},{8,0},{12,4},{16,8},{20,12},{24,16},{28,20},{32,56},... | collective-permute-start | bytes 442376 | tf_op jit(solution)/shard_map/ppermute | solution.py:117
  496.2 16.7 %collective-permute-start.20 = (bf16[8,72,128]{2,1,0:T(8,128)(2,1)S(1)}, bf16[8,72,128]{2,1,0:T(8,128)(2,1)S(1)}, u32[]{:S(2)}, u32[]{:S(2)}) collective-permute-start(bf16[8,72,128]{2,1,0:T(8,128)(2,1)S(1)} %get-tuple-element.48), channel_id=1, source_target_pairs={{0,16},{4,20},{8,24},{12,28},{16,0},{20,4},{24,8},{28,12},{32,48},... | collective-permute-start | bytes 442376 | tf_op jit(solution)/shard_map/ppermute | solution.py:117
  496.7 16.1 %collective-permute-start.19 = (bf16[8,72,128]{2,1,0:T(8,128)(2,1)S(1)}, bf16[8,72,128]{2,1,0:T(8,128)(2,1)S(1)}, u32[]{:S(2)}, u32[]{:S(2)}) collective-permute-start(bf16[8,72,128]{2,1,0:T(8,128)(2,1)S(1)} %get-tuple-element.46), channel_id=1, source_target_pairs={{0,8},{4,12},{8,16},{12,20},{16,24},{20,28},{24,0},{28,4},{32,40},... | collective-permute-start | bytes 442376 | tf_op jit(solution)/shard_map/ppermute | solution.py:117
  504.5 15.0 %all-to-all-start.6 = ((bf16[8,72,128]{2,1,0:T(8,128)(2,1)}), bf16[8,72,128]{2,1,0:T(8,128)(2,1)S(1)}, u32[]{:S(2)}, u32[]{:S(2)}) async-start(bf16[8,72,128]{2,1,0:T(8,128)(2,1)} %fusion.94), calls=%async_computation.6 | async-start | bytes 294912 | tf_op jit(solution)/shard_map/all_to_all | solution.py:91
  511.7 21.8 %copy-start.1 = (bf16[768,768]{1,0:T(8,128)(2,1)S(1)}, bf16[768,768]{1,0:T(8,128)(2,1)}, u32[]{:S(2)}) copy-start(bf16[768,768]{1,0:T(8,128)(2,1)} %param.20) | copy-start | bytes 3538948
  519.5 12.6 %all-to-all-start.5 = ((bf16[8,72,128]{2,1,0:T(8,128)(2,1)}), bf16[8,72,128]{2,1,0:T(8,128)(2,1)S(1)}, u32[]{:S(2)}, u32[]{:S(2)}) async-start(bf16[8,72,128]{2,1,0:T(8,128)(2,1)} %fusion.97), calls=%async_computation.5 | async-start | bytes 294912 | tf_op jit(solution)/shard_map/all_to_all | solution.py:91
  (5 other events, 4.6 us)
